TPU v7x, 128 devices: a whole 4x4x4 slice. The times are simulated.
128 devices in a mesh: dp: 16 (over z, y), tensor: 8 (over x, core).
Axes of the slice: x: 4, y: 4, z: 4, core: 2. Of those that a mesh axis runs over, the one named last changes fastest.
Arguments:
- acts: bfloat16 [24576, 6144], P('dp', 'tensor'), may hold values from -600 to 600, as said below
- grads_out: bfloat16 [24576, 24576], P('dp', 'tensor'), may hold values from -600 to 600, as said below
- sketch_in: bfloat16 [6144, 256], P('tensor'), may hold values from -0.078125 to 0.078125
- sketch_out: bfloat16 [24576, 256], P('tensor'), may hold values from -0.0390625 to 0.0390625
- weight_grad: float32 [6144, 24576], P('dp', 'tensor'), may hold values from -6 to 6
Outputs:
- precond: float32 [6144, 24576], P('dp', 'tensor')
Inputs may be any that keep to these rules, and one draw needn't show every extreme that they name: acts: rows and columns of varying scale. grads_out: rows and columns of varying scale.
All inputs are finite; a program needn't handle non-finite values.
Results may differ from a plain program's by a relative error of at most 0.0015.
Values sent between devices are 32-bit elements; how exact they have to be, the bound alone decides.
No kernel may reach another device: no remote copies, remote signals or barrier semaphores. Data moves between devices by JAX's collectives and lax.ppermute only.
A program may use at most 128 MiB of HBM per device.

v0:
```python
import functools

import jax
import jax.numpy as jnp
from jax import lax
from jax.experimental import pallas as pl
from jax.experimental.pallas import tpu as pltpu
from jax.sharding import PartitionSpec as P

D = 6144
FF = 24576
R = 256
TILE = 1024
BLOCK = 64
VMEM_LIMIT = 48 * 1024 * 1024
VMEM_MOST = 60 * 1024 * 1024

DAMPING = 0.1


def ring(kind, step):
    if kind == "y":
        return [(i, i // 4 * 4 + (i % 4 + step) % 4) for i in range(16)]
    if kind == "z":
        return [(i, (i // 4 + step) % 4 * 4 + i % 4) for i in range(16)]
    return [(i, (i // 2 + step) % 4 * 2 + i % 2) for i in range(8)]


def send(value, kind, step):
    return lax.ppermute(value, "tensor" if kind == "x" else "dp", ring(kind, step))


def swap_cores(value):
    return lax.ppermute(value, "tensor", [(i, i ^ 1) for i in range(8)])


def place(kind):
    if kind == "y":
        return lax.axis_index("dp") % 4
    if kind == "z":
        return lax.axis_index("dp") // 4
    return lax.axis_index("tensor") // 2


def rows(value, index, count):
    return lax.dynamic_slice_in_dim(value, index * count, count, 0)


def scatter_blocks(blocks, kind):
    two, one, three = (send(blocks[step], kind, step) for step in (2, 1, 3))
    return (blocks[0] + two) + (one + three)


def scatter_four(value, kind):
    here, count = place(kind), value.shape[0] // 4
    return scatter_blocks([rows(value, (here + step) % 4, count) for step in range(4)], kind)


def gather_four(value, kind):
    two, one, three = (send(value, kind, step) for step in (2, 1, 3))
    return assemble((value, one, two, three), place(kind))


def assemble(parts, here):
    count = parts[0].shape[0]
    whole = jnp.zeros((4 * count,) + parts[0].shape[1:], parts[0].dtype)
    for step, part in enumerate(parts):
        whole = lax.dynamic_update_slice_in_dim(whole, part, (here - step) % 4 * count, 0)
    return whole


def scatter_dp(blocks):
    first, second = scatter_blocks(blocks[:4], "y"), scatter_blocks(blocks[4:], "z")
    return jnp.concatenate([scatter_four(first, "z"), scatter_four(second, "y")])


def store_blocks(blocks, places, columns, value, stride=16):
    y, z = places[2], places[3]
    for step in range(4):
        for other in range(4):
            to = slice(8 * other, 8 * other + 8)
            at = (4 * other + lax.rem(y + step, 4)) * stride
            blocks[step][to, columns] = value[pl.ds(pl.multiple_of(at, 8), 8), :]
            at = (4 * lax.rem(z + step, 4) + other) * stride + 8
            blocks[4 + step][to, columns] = value[pl.ds(pl.multiple_of(at, 8), 8), :]


def tensor_chunk():
    index = lax.axis_index("tensor")
    return index % 2 * 4 + index // 2


def scatter_tensor(value):
    core, half = lax.axis_index("tensor") % 2, value.shape[0] // 2
    other = swap_cores(rows(value, 1 - core, half))
    return scatter_four(rows(value, core, half) + other, "x")


def gather_cores(value):
    core = lax.axis_index("tensor") % 2
    other = swap_cores(value)
    low = jnp.where(core == 0, value, other)
    high = jnp.where(core == 0, other, value)
    return jnp.concatenate([low, high])


def gather_tensor(value):
    return gather_cores(gather_four(value, "x"))


def gather_rows(piece):
    moves = []
    for d in range(16):
        for t in range(8):
            moves.append((d * 8 + t, (2 * t + d // 8) * 8 + 2 * (d % 4) + d % 8 // 4))
    return gather_tensor(lax.ppermute(piece, ("dp", "tensor"), moves))


def split(value):
    high = value.astype(jnp.bfloat16)
    return high, (value - high.astype(jnp.float32)).astype(jnp.bfloat16)


def product(left, right, dims):
    (lh, ll), (rh, rl) = left, right
    (along_left,), (along_right,) = dims
    return lax.dot_general(
        jnp.concatenate([lh, lh, ll], axis=along_left),
        jnp.concatenate([rh, rl, rh], axis=along_right),
        (dims, ((), ())),
        preferred_element_type=jnp.float32,
    )


def call(kernel, out_shape, vmem=VMEM_LIMIT, **options):
    return pl.pallas_call(
        kernel,
        out_shape=out_shape,
        compiler_params=pltpu.CompilerParams(vmem_limit_bytes=vmem),
        **options,
    )


def array(*shape):
    return jax.ShapeDtypeStruct(shape, jnp.float32)


def sketch_kernel(core, grads, acts, sketch_out, sketch_in, out, squares, total_grad, total_act):
    step = pl.program_id(0)
    some = zip((grads, acts), (sketch_out, sketch_in), (total_grad, total_act))
    for i, (value, sketch, total) in enumerate(some):

        @pl.when(step == 0)
        def _():
            total[...] = jnp.zeros_like(total)

        out[:, i * R : i * R + R] = jnp.dot(
            value[...], sketch[...], preferred_element_type=jnp.float32
        )
        count, columns = value.shape
        for low in range(0, columns, 256):
            sums = jnp.zeros((16, 256), jnp.float32)
            for row in range(0, count, 16):
                sums += jnp.square(value[row : row + 16, low : low + 256].astype(jnp.float32))
            total[:, low : low + 256] += sums

        @pl.when(step == pl.num_programs(0) - 1)
        def _():
            whole = jnp.sum(total[...], keepdims=True)
            squares[8 * i : 8 * i + 8, :] = jnp.broadcast_to(whole, (8, 128))


def sketches(half, grads, acts, sketch_out, sketch_in):
    count = grads.shape[0] // 2
    step = 384
    steps = count // step
    tile = lambda columns: pl.BlockSpec((step, columns), lambda i, h: (h[0] * steps + i, 0))
    whole = lambda value: pl.BlockSpec(value.shape, lambda i, h: (0, 0))
    grid_spec = pltpu.PrefetchScalarGridSpec(
        num_scalar_prefetch=1,
        grid=(steps,),
        in_specs=[
            tile(grads.shape[1]),
            tile(acts.shape[1]),
            whole(sketch_out),
            whole(sketch_in),
        ],
        out_specs=[
            pl.BlockSpec((step, 2 * R), lambda i, h: (i, 0)),
            pl.BlockSpec((16, 128), lambda i, h: (0, 0)),
        ],
        scratch_shapes=[
            pltpu.VMEM((16, grads.shape[1]), jnp.float32),
            pltpu.VMEM((16, acts.shape[1]), jnp.float32),
        ],
    )
    return call(
        sketch_kernel,
        [array(count, 2 * R), array(16, 128)],
        vmem=VMEM_MOST,
        grid_spec=grid_spec,
        name="sketches",
    )(half.astype(jnp.int32).reshape(1), grads, acts, sketch_out, sketch_in)


LAST = ((1,), (1,))
INNER = ((1,), (0,))


def flip_halves(core, own, other, flipped):
    half = own.shape[0]
    flipped[:, pl.ds(pl.multiple_of(core * half, 128), half)] = own[...].T
    flipped[:, pl.ds(pl.multiple_of((1 - core) * half, 128), half)] = other[...].T


def ranges_kernel(
    tokens_all, places, own, other, grads, acts, sq_one, sq_two, *refs
):
    blocks, (flipped, rounded, range_act, work) = refs[:8], refs[8:]
    step = pl.program_id(0)
    columns = grads.shape[1]
    whole = pl.num_programs(0) * columns

    @pl.when(step == 0)
    def _():
        half = own.shape[0]
        flipped[:, pl.ds(pl.multiple_of(places[1] * half, 128), half)] = own[...].T
        flipped[:, pl.ds(pl.multiple_of((1 - places[1]) * half, 128), half)] = other[...].T
        rounded[...] = flipped[...].astype(jnp.bfloat16)

    part = jnp.dot(rounded[:R, :], grads[...], preferred_element_type=jnp.float32)
    work[...] = part * (1.0 / tokens_all)
    store_blocks(blocks, places, pl.ds(pl.multiple_of(step * columns, 128), columns), work)

    @pl.when(step == pl.num_programs(0) - 1)
    def _():
        cores = []
        for low in (0, R):
            some = flipped[pl.ds(pl.multiple_of(low + places[0] * 32, 32), 32), :]
            core = product(split(flipped[low : low + R, :]), split(some), LAST)
            cores.append(core * (1.0 / tokens_all))
        lane = lax.broadcasted_iota(jnp.int32, (R, 64), 1)
        squares = sq_one[...] + sq_two[...]
        traces = jnp.where(lane == 0, squares[0:1, 0:1], 0.0)
        traces = jnp.where(lane == 1, squares[8:9, 0:1], traces)
        rest = jnp.concatenate(cores + [traces], axis=1)
        work[:, :128] = rest
        store_blocks(blocks, places, pl.ds(whole, 128), work.at[:, :128])
        part = jnp.dot(rounded[R:, :], acts[...], preferred_element_type=jnp.float32)
        range_act[...] = part.T * (1.0 / tokens_all)
        for i in range(3):
            to = pl.ds(whole + 128 + i * R, R)
            store_blocks(blocks, places, to, range_act.at[16 * i :, :], 48)


def ranges(places, own, other, grads, acts, sq_one, sq_two, tokens_all):
    count, columns = grads.shape
    fixed = lambda shape: pl.BlockSpec(shape, lambda j, c: (0, 0))
    total = columns + 128 + 3 * R
    grid_spec = pltpu.PrefetchScalarGridSpec(
        num_scalar_prefetch=1,
        grid=(columns // TILE,),
        in_specs=[
            fixed(own.shape),
            fixed(other.shape),
            pl.BlockSpec((count, TILE), lambda j, c: (0, j)),
            fixed(acts.shape),
            fixed((16, 128)),
            fixed((16, 128)),
        ],
        out_specs=[fixed((R // 8, total))] * 8,
        scratch_shapes=[
            pltpu.VMEM((2 * R, count), jnp.float32),
            pltpu.VMEM((2 * R, count), jnp.bfloat16),
            pltpu.VMEM((acts.shape[1], R), jnp.float32),
            pltpu.VMEM((R, TILE), jnp.float32),
        ],
    )
    return call(
        functools.partial(ranges_kernel, tokens_all),
        [array(R // 8, total)] * 8,
        grid_spec=grid_spec,
        name="ranges",
    )(places, own, other, grads, acts, sq_one, sq_two)


def left_kernel(places, rows_act, weight, *refs):
    blocks, (high, low, work) = refs[:8], refs[8:]
    step = pl.program_id(0)
    columns = weight.shape[1]

    @pl.when(step == 0)
    def _():
        high[...], low[...] = split(rows_act[...].T)

    work[...] = product((high[...], low[...]), split(weight[...]), INNER)
    store_blocks(blocks, places, pl.ds(pl.multiple_of(step * columns, 128), columns), work)


def left_products(places, rows_act, weight):
    count, columns = weight.shape
    grid_spec = pltpu.PrefetchScalarGridSpec(
        num_scalar_prefetch=1,
        grid=(columns // TILE,),
        in_specs=[
            pl.BlockSpec((count, R), lambda j, c: (0, 0)),
            pl.BlockSpec((count, TILE), lambda j, c: (0, j)),
        ],
        out_specs=[pl.BlockSpec((R // 8, columns), lambda j, c: (0, 0))] * 8,
        scratch_shapes=[pltpu.VMEM((R, count), jnp.bfloat16)] * 2
        + [pltpu.VMEM((R, TILE), jnp.float32)],
    )
    return call(
        left_kernel, [array(R // 8, columns)] * 8, grid_spec=grid_spec, name="left_products"
    )(places, rows_act, weight)


def right_kernel(whole, *refs):
    extra, (weight, left, sums, both) = refs[:6], refs[6:]

    @pl.when(pl.program_id(0) == 0)
    def _():
        sums[...] = jnp.zeros_like(sums)
        both[...] = jnp.zeros_like(both)
        blocks = [jnp.concatenate([extra[i][...], extra[i + 1][...]], axis=1) for i in (0, 2, 4)]
        pieces = split(jnp.concatenate(blocks))
        gram = product(pieces, pieces, ((0,), (0,)))
        for i in range(8):
            sums[i * 112 + 80 : i * 112 + 112, :] = gram[i * 32 : i * 32 + 32]

    ranges = split(whole[...])
    right = product(split(weight[...]), ranges, LAST)
    gram = product(ranges, ranges, LAST)
    for i in range(8):
        at = i * 112
        sums[at : at + 48, :] += right[i * 48 : i * 48 + 48]
        sums[at + 48 : at + 80, :] += gram[i * 32 : i * 32 + 32]
    both[...] += product(split(left[...]), ranges, LAST)


def right_products(gathered, weight, left):
    count, columns = weight.shape
    extra = lambda i: pl.BlockSpec((R, 128), lambda j: (0, columns // 128 + 1 + i))
    return call(
        right_kernel,
        [array(896, R), array(16, R)],
        grid=(columns // TILE,),
        in_specs=[pl.BlockSpec((R, TILE), lambda j: (0, j))]
        + [extra(i) for i in range(6)]
        + [
            pl.BlockSpec((count, TILE), lambda j: (0, j)),
            pl.BlockSpec((16, TILE), lambda j: (0, j)),
        ],
        out_specs=[
            pl.BlockSpec((896, R), lambda j: (0, 0)),
            pl.BlockSpec((16, R), lambda j: (0, 0)),
        ],
        vmem=VMEM_MOST,
        name="right_products",
    )(*[gathered] * 7, weight, left)


def pack_kernel(right, out):
    total = right[184:200, :]
    for i in range(1, 8):
        total += right[i * 200 + 184 : i * 200 + 200, :]
    for d in range(16):
        out[16 * d : 16 * d + 16, :] = total


def pack(right):
    whole = pl.BlockSpec(memory_space=pltpu.VMEM)
    return call(pack_kernel, array(R, R), in_specs=[whole], out_specs=whole, name="pack")(right)


def exact(left, right, dims):
    return lax.dot_general(
        left,
        right,
        (dims, ((), ())),
        precision=lax.Precision.HIGHEST,
        preferred_element_type=jnp.float32,
    )


def spread(value):
    return jnp.broadcast_to(value, (8, 2 * BLOCK))


def eliminate(matrices):
    sub = lax.broadcasted_iota(jnp.int32, (8, 2 * BLOCK), 0)
    count = BLOCK // 8
    groups = [[m[8 * i : 8 * i + 8] for i in range(count)] for m in matrices]
    for at in range(count):
        k = 8 * at
        for group in groups:
            tile = group[at]
            lines = [spread(tile[j : j + 1]) for j in range(8)]
            pivot = {
                (j, l): spread(lines[j][:, k + l : k + l + 1])
                for j in range(8)
                for l in range(j, 8)
            }
            scaled, factor = [], {}
            for j in range(8):
                inverse = 1.0 / pivot[j, j]
                scaled.append(lines[j] * inverse)
                for l in range(j + 1, 8):
                    factor[j, l] = pivot[j, l] * inverse
                    for m in range(l, 8):
                        pivot[l, m] = pivot[l, m] - factor[j, l] * pivot[j, m]
                    lines[l] = lines[l] - factor[j, l] * lines[j]
            for i in range(at + 1, count):
                value, sums, columns = group[i], None, []
                for j in range(8):
                    column = spread(value[:, k + j : k + j + 1])
                    for q in range(j):
                        column = column - columns[q] * factor[q, j]
                    columns.append(column)
                    term = column * scaled[j]
                    sums = term if sums is None else sums + term
                group[i] = value - sums
            for j in range(8):
                tile = jnp.where(sub == j, lines[j] * lax.rsqrt(pivot[j, j]), tile)
            group[at] = tile
    return [jnp.concatenate(group, axis=0) for group in groups]


def lower_inverses(work, outs):
    row = lax.broadcasted_iota(jnp.int32, (BLOCK, BLOCK), 0)
    column = lax.broadcasted_iota(jnp.int32, (BLOCK, BLOCK), 1)
    identity = jnp.where(row == column, 1.0, 0.0)
    for low in range(0, R, BLOCK):
        high = low + BLOCK
        done = eliminate(
            [jnp.concatenate([w[low:high, low:high], identity], axis=1) for w in work]
        )
        for w, corner, out in zip(work, done, outs):
            corner = jnp.where(row >= column, corner[:, BLOCK:], 0.0)
            line = exact(corner, w[low:high, :], INNER)
            out[low:high, :] = line[:, R:]
            if high < R:
                w[high:, :] -= exact(line[:, high:R], line, ((0,), (0,)))


def factor_kernel(counts, right, inverse_act, inverse_grad, scale, *work):
    trace_grad, trace_act = jnp.zeros((1, 1)), jnp.zeros((1, 1))
    for i in range(8):
        at = i * 200 + 176
        trace_grad += right[at : at + 1, 64:65]
        trace_act += right[at : at + 1, 65:66]
    damp_grad = DAMPING * trace_grad / counts[0]
    damp_act = DAMPING * trace_act / counts[1]
    scale[...] = jnp.broadcast_to(1.0 / (damp_act * damp_grad), (8, 128))
    row = lax.broadcasted_iota(jnp.int32, (R, R), 0)
    column = lax.broadcasted_iota(jnp.int32, (R, R), 1)
    identity = jnp.where(row == column, 1.0, 0.0)
    for w in work:
        w[:, R:] = identity
    for i in range(8):
        at, here = slice(i * 32, i * 32 + 32), i * 200
        work[0][at, :R] = damp_act * right[here + 144 : here + 176, :] + right[here + 80 : here + 112, :]
        work[1][at, :R] = damp_grad * right[here + 112 : here + 144, :] + right[here + 48 : here + 80, :]
    lower_inverses(work, (inverse_act, inverse_grad))


def factors(right, counts):
    whole = pl.BlockSpec(memory_space=pltpu.VMEM)
    return call(
        functools.partial(factor_kernel, counts),
        [array(R, R), array(R, R), array(8, 128)],
        in_specs=[whole],
        out_specs=[whole] * 3,
        scratch_shapes=[pltpu.VMEM((R, 2 * R), jnp.float32)] * 2,
        name="factors",
    )(right)


def applied(value, inverse):
    pieces = split(inverse)
    value = product(split(value), pieces, LAST)
    return product(split(value), pieces, INNER)


def last_kernel(
    left_sums, weight, range_grad, right, both, rows_act, inverse_act, inverse_grad, scale, out, sums, *pieces
):
    @pl.when(pl.program_id(0) == 0)
    def _():
        for i in range(8):
            sums[i * 48 : i * 48 + 48, :] = right[i * 200 : i * 200 + 48, :]
        solved = applied(rows_act[...], inverse_act[...])
        pieces[0][...], pieces[1][...] = split(solved)
        rest = sums[...] - product(split(solved), split(both[...]), INNER)
        pieces[2][...], pieces[3][...] = split(applied(rest, inverse_grad[...]))

    left = product((pieces[0][...], pieces[1][...]), split(left_sums[...]), INNER)
    range_pieces = split(range_grad[...])
    update = left + product((pieces[2][...], pieces[3][...]), range_pieces, INNER)
    out[...] = (weight[...] - update) * scale[0:1, 0:1]


def last_update(left_sums, weight, range_grad, *rest):
    count, columns = weight.shape
    return call(
        last_kernel,
        array(count, columns),
        grid=(columns // TILE,),
        in_specs=[
            pl.BlockSpec((R, TILE), lambda j: (0, j)),
            pl.BlockSpec((count, TILE), lambda j: (0, j)),
            pl.BlockSpec((R, TILE), lambda j: (0, j)),
        ]
        + [pl.BlockSpec(value.shape, lambda j: (0, 0)) for value in rest],
        out_specs=pl.BlockSpec((count, TILE), lambda j: (0, j)),
        scratch_shapes=[pltpu.VMEM((count, R), jnp.float32)]
        + [pltpu.VMEM((count, R), jnp.bfloat16)] * 4,
        name="last_update",
    )(left_sums, weight, range_grad, *rest)


def hand_over_dp(value):
    return lax.all_to_all(value, "dp", 0, 0, tiled=True)


def body(acts, grads_out, sketch_in, sketch_out, weight_grad):
    tokens_all = acts.shape[0] * lax.axis_size("dp")
    columns = weight_grad.shape[1]
    core_id = lax.axis_index("tensor") % 2
    places = jnp.stack([tensor_chunk(), core_id, place("y"), place("z")]).astype(jnp.int32)
    width = R // 8

    part, sq_one = sketches(1 - core_id, grads_out, acts, sketch_out, sketch_in)
    other = swap_cores(part)
    part, sq_two = sketches(core_id, grads_out, acts, sketch_out, sketch_in)
    own = gather_four(scatter_four(part + other, "x"), "x")
    other = swap_cores(own)

    piece = scatter_dp(
        ranges(places, own, other, grads_out, acts, sq_one, sq_two, tokens_all)
    )
    gathered = lax.all_gather(piece, "dp", axis=0, tiled=True)

    at = columns + 128
    piece = jnp.concatenate([piece[:, at + i * R : at + i * R + R] for i in range(3)])
    rows_act = gather_rows(piece)

    piece = scatter_dp(left_products(places, rows_act, weight_grad))
    left_sums = lax.all_gather(piece, "dp", axis=0, tiled=True)

    part, both = right_products(gathered, weight_grad, piece)
    part = scatter_tensor(part)
    extra = gathered[:, columns:at]
    cores = extra[:, : 2 * width].T
    rest = jnp.pad(extra[:8], ((0, 0), (0, R - 128)))
    part = jnp.concatenate([part, cores, rest, both])
    right = gather_tensor(part)
    both = lax.all_to_all(pack(right), "dp", 0, 0, tiled=True)

    counts = (float(tokens_all * FF), float(tokens_all * D))
    inverse_act, inverse_grad, scale = factors(right, counts)
    return last_update(
        left_sums, weight_grad, gathered, right, both, rows_act, inverse_act, inverse_grad, scale
    )


def solution(mesh):
    return jax.shard_map(
        body,
        mesh=mesh,
        in_specs=(
            P("dp", "tensor"),
            P("dp", "tensor"),
            P("tensor", None),
            P("tensor", None),
            P("dp", "tensor"),
        ),
        out_specs=P("dp", "tensor"),
        check_vma=False,
    )
```

profile of v0, /device:TPU:1, one launch (start us, length us, event | category | flops | bytes accessed | tf_op | source)
XLA Modules:
  0.0 292.3 jit_solution(3372636581073842731)
XLA Ops:
  6.5 6.4 %sketches.3 = (f32[768,512]{1,0:T(8,128)}, f32[16,128]{1,0:T(8,128)}) custom-call(s32[1]{0:T(128)} %bitcast.4.core, bf16[1536,3072]{1,0:T(8,128)(2,1)} %grads.5, bf16[1536,768]{1,0:T(8,128)(2,1)} %acts.5, bf16[3072,256]{1,0:T(8,128)(2,1)} %sketch_out.3, bf16[768,256]{1,0:T(8,128)(2,1)} %sketch_in.3), custom_call_target="tpu_custom_call" | custom-call | tf_op jit(solution)/shard_map/sketches/pallas_call | solution.py:197
  12.9 1.4 collective-permute-start
  14.3 6.3 %sketches.2 = (f32[768,512]{1,0:T(8,128)}, f32[16,128]{1,0:T(8,128)}) custom-call(s32[1]{0:T(128)} %bitcast.1.core, bf16[1536,3072]{1,0:T(8,128)(2,1)} %grads.5, bf16[1536,768]{1,0:T(8,128)(2,1)} %acts.5, bf16[3072,256]{1,0:T(8,128)(2,1)} %sketch_out.3, bf16[768,256]{1,0:T(8,128)(2,1)} %sketch_in.3), custom_call_target="tpu_custom_call" | custom-call | tf_op jit(solution)/shard_map/sketches/pallas_call | solution.py:197
  20.7 1.8 add.320
  22.4 1.1 copy-done.5
  23.6 2.9 %collective-permute-start.1 = (f32[192,512]{1,0:T(8,128)S(1)}, f32[192,512]{1,0:T(8,128)S(1)}, u32[]{:S(2)}, u32[]{:S(2)}) collective-permute-start(f32[192,512]{1,0:T(8,128)S(1)} %get-tuple-element.59), channel_id=1, source_target_pairs={{0,4},{1,5},{2,6},{3,7},{4,0},{5,1},{6,2},{7,3},{8,12},{9,13},{10,... | collective-permute-start | bytes 1179656 | tf_op jit(solution)/shard_map/ppermute | solution.py:30
  28.0 7.9 %collective-permute-done.1 = f32[192,512]{1,0:T(8,128)S(1)} collective-permute-done((f32[192,512]{1,0:T(8,128)S(1)}, f32[192,512]{1,0:T(8,128)S(1)}, u32[]{:S(2)}, u32[]{:S(2)}) %collective-permute-start.1) | collective-permute-done | bytes 393248 | tf_op jit(solution)/shard_map/ppermute | solution.py:30
  35.9 8.6 %collective-permute-done.3 = f32[192,512]{1,0:T(8,128)S(1)} collective-permute-done((f32[192,512]{1,0:T(8,128)S(1)}, f32[192,512]{1,0:T(8,128)S(1)}, u32[]{:S(2)}, u32[]{:S(2)}) %collective-permute-start.3) | collective-permute-done | bytes 393248 | tf_op jit(solution)/shard_map/ppermute | solution.py:30
  44.9 1.2 constant_dynamic-update-slice_fusion.11
  46.1 1.4 collective-permute-start.4
  47.5 2.5 collective-permute-start.5
  49.9 1.1 collective-permute-start.6
  51.1 6.2 %collective-permute-done.4 = f32[192,512]{1,0:T(8,128)S(1)} collective-permute-done((f32[192,512]{1,0:T(8,128)S(1)}, f32[192,512]{1,0:T(8,128)S(1)}, u32[]{:S(2)}, u32[]{:S(2)}) %collective-permute-start.4) | collective-permute-done | bytes 393248 | tf_op jit(solution)/shard_map/ppermute | solution.py:30
  57.3 9.8 %collective-permute-done.5 = f32[192,512]{1,0:T(8,128)S(1)} collective-permute-done((f32[192,512]{1,0:T(8,128)S(1)}, f32[192,512]{1,0:T(8,128)S(1)}, u32[]{:S(2)}, u32[]{:S(2)}) %collective-permute-start.5) | collective-permute-done | bytes 393248 | tf_op jit(solution)/shard_map/ppermute | solution.py:30
  67.2 1.4 collective-permute-start.7
  68.7 3.1 %collective-permute-done.7.other = f32[768,512]{1,0:T(8,128)} collective-permute-done((f32[768,512]{1,0:T(8,128)S(1)}, f32[768,512]{1,0:T(8,128)}, u32[]{:S(2)}, u32[]{:S(2)}) %collective-permute-start.7) | collective-permute-done | bytes 1572896 | tf_op jit(solution)/shard_map/ppermute | solution.py:34
  71.8 12.2 %ranges.1 = (f32[32,3968]{1,0:T(8,128)S(1)}, f32[32,3968]{1,0:T(8,128)}, f32[32,3968]{1,0:T(8,128)}, f32[32,3968]{1,0:T(8,128)}, f32[32,3968]{1,0:T(8,128)S(1)},...) custom-call(s32[4]{0:T(128)S(1)} %pad_add_fusion.places, ...), custom_call_target="tpu_custom_call" | custom-call | tf_op jit(solution)/shard_map/ranges/pallas_call | solution.py:279
  85.6 2.9 collective-permute-start.8
  88.9 2.3 collective-permute-start.10
  91.2 3.6 %collective-permute-start.14 = (f32[32,3968]{1,0:T(8,128)}, f32[32,3968]{1,0:T(8,128)S(1)}, u32[]{:S(2)}, u32[]{:S(2)}) collective-permute-start(f32[32,3968]{1,0:T(8,128)} %copy-done.4), channel_id=1, source_target_pairs={{0,64},{8,72},{16,80},{24,88},{32,96},{40,104},{48,112},{56,120},{... | collective-permute-start | bytes 1523720 | tf_op jit(solution)/shard_map/ppermute | solution.py:30
  95.6 4.6 %collective-permute-done.8 = f32[32,3968]{1,0:T(8,128)S(1)} collective-permute-done((f32[32,3968]{1,0:T(8,128)}, f32[32,3968]{1,0:T(8,128)S(1)}, u32[]{:S(2)}, u32[]{:S(2)}) %collective-permute-start.8) | collective-permute-done | bytes 507936 | tf_op jit(solution)/shard_map/ppermute | solution.py:30
  100.1 3.8 %collective-permute-start.16 = (f32[32,3968]{1,0:T(8,128)S(1)}, f32[32,3968]{1,0:T(8,128)S(1)}, u32[]{:S(2)}, u32[]{:S(2)}) collective-permute-start(f32[32,3968]{1,0:T(8,128)S(1)} %get-tuple-element.41), channel_id=1, source_target_pairs={{0,96},{8,104},{16,112},{24,120},{32,0},{40,8},{48,16},{56,24},{64... | collective-permute-start | bytes 1523720 | tf_op jit(solution)/shard_map/ppermute | solution.py:30
  103.9 7.8 %collective-permute-done.9 = f32[32,3968]{1,0:T(8,128)S(1)} collective-permute-done((f32[32,3968]{1,0:T(8,128)}, f32[32,3968]{1,0:T(8,128)S(1)}, u32[]{:S(2)}, u32[]{:S(2)}) %collective-permute-start.9) | collective-permute-done | bytes 507936 | tf_op jit(solution)/shard_map/ppermute | solution.py:30
  111.8 3.9 %collective-permute-start.11 = (f32[8,3968]{1,0:T(8,128)S(1)}, f32[8,3968]{1,0:T(8,128)S(1)}, u32[]{:S(2)}, u32[]{:S(2)}) collective-permute-start(f32[8,3968]{1,0:T(8,128)S(1)} %get-tuple-element.65), channel_id=1, source_target_pairs={{0,64},{8,72},{16,80},{24,88},{32,96},{40,104},{48,112},{56,120},{... | collective-permute-start | bytes 380936 | tf_op jit(solution)/shard_map/ppermute | solution.py:30
  117.3 1.5 collective-permute-done.15
  119.0 2.2 collective-permute-start.19
  121.2 2.1 collective-permute-done.13
  124.3 1.1 collective-permute-done.19
  125.4 2.6 collective-permute-done.18
  128.8 3.8 %collective-permute-start.20 = (f32[48,256]{1,0:T(8,128)S(1)}, f32[48,256]{1,0:T(8,128)S(1)}, u32[]{:S(2)}, u32[]{:S(2)}) collective-permute-start(f32[48,256]{1,0:T(8,128)S(1)} %pad_maximum_fusion.4), channel_id=1, source_target_pairs={{0,0},{1,16},{2,32},{3,48},{4,64},{5,80},{6,96},{7,112},{8,2},{9,1... | collective-permute-start | bytes 147464 | tf_op jit(solution)/shard_map/ppermute | solution.py:116
  132.6 2.2 collective-permute-done.20
  134.8 6.0 %collective-permute-start.23 = (f32[48,256]{1,0:T(8,128)S(1)}, f32[48,256]{1,0:T(8,128)S(1)}, u32[]{:S(2)}, u32[]{:S(2)}) collective-permute-start(f32[48,256]{1,0:T(8,128)S(1)} %collective-permute-done.20), channel_id=1, source_target_pairs={{0,6},{1,7},{2,0},{3,1},{4,2},{5,3},{6,4},{7,5},{8,14},{9,15},{10,... | collective-permute-start | bytes 147464 | tf_op jit(solution)/shard_map/ppermute | solution.py:30
  142.2 3.6 %collective-permute-done.21 = f32[48,256]{1,0:T(8,128)S(1)} collective-permute-done((f32[48,256]{1,0:T(8,128)S(1)}, f32[48,256]{1,0:T(8,128)S(1)}, u32[]{:S(2)}, u32[]{:S(2)}) %collective-permute-start.21) | collective-permute-done | bytes 49184 | tf_op jit(solution)/shard_map/ppermute | solution.py:30
  145.8 2.7 collective-permute-start.24
  148.5 1.1 collective-permute-done.24
  149.7 5.6 %left_products.1 = (f32[32,3072]{1,0:T(8,128)S(1)}, f32[32,3072]{1,0:T(8,128)S(1)}, f32[32,3072]{1,0:T(8,128)S(1)}, f32[32,3072]{1,0:T(8,128)S(1)}, f32[32,3072]...) custom-call(s32[4]{0:T(128)S(1)} %pad_add_fusion.places, ...), custom_call_target="tpu_custom_call" | custom-call | tf_op jit(solution)/shard_map/left_products/pallas_call | solution.py:313
  156.1 1.4 collective-permute-start.26
  157.6 2.0 collective-permute-start.27
  159.6 1.1 collective-permute-start.31
  160.7 2.8 collective-permute-start.32
  163.5 6.3 %collective-permute-done.25 = f32[32,3072]{1,0:T(8,128)S(1)} collective-permute-done((f32[32,3072]{1,0:T(8,128)S(1)}, f32[32,3072]{1,0:T(8,128)S(1)}, u32[]{:S(2)}, u32[]{:S(2)}) %collective-permute-start.25) | collective-permute-done | bytes 393248 | tf_op jit(solution)/shard_map/ppermute | solution.py:30
  169.9 7.1 %collective-permute-start.33 = (f32[32,3072]{1,0:T(8,128)S(1)}, f32[32,3072]{1,0:T(8,128)S(1)}, u32[]{:S(2)}, u32[]{:S(2)}) collective-permute-start(f32[32,3072]{1,0:T(8,128)S(1)} %get-tuple-element.49), channel_id=1, source_target_pairs={{0,96},{8,104},{16,112},{24,120},{32,0},{40,8},{48,16},{56,24},{64... | collective-permute-start | bytes 1179656 | tf_op jit(solution)/shard_map/ppermute | solution.py:30
  177.0 7.7 %collective-permute-done.26 = f32[32,3072]{1,0:T(8,128)S(1)} collective-permute-done((f32[32,3072]{1,0:T(8,128)S(1)}, f32[32,3072]{1,0:T(8,128)S(1)}, u32[]{:S(2)}, u32[]{:S(2)}) %collective-permute-start.26) | collective-permute-done | bytes 393248 | tf_op jit(solution)/shard_map/ppermute | solution.py:30
  184.8 1.8 collective-permute-start.28
  186.6 6.1 %collective-permute-start.30 = (f32[8,3072]{1,0:T(8,128)S(1)}, f32[8,3072]{1,0:T(8,128)S(1)}, u32[]{:S(2)}, u32[]{:S(2)}) collective-permute-start(f32[8,3072]{1,0:T(8,128)S(1)} %get-tuple-element.72), channel_id=1, source_target_pairs={{0,96},{8,104},{16,112},{24,120},{32,0},{40,8},{48,16},{56,24},{64... | collective-permute-start | bytes 294920 | tf_op jit(solution)/shard_map/ppermute | solution.py:30
  193.2 2.4 collective-permute-done.33
  195.8 2.6 collective-permute-start.34
  200.9 1.6 collective-permute-done.36
  202.5 2.8 collective-permute-done.35
  206.1 8.3 %right_products.1 = (f32[896,256]{1,0:T(8,128)}, f32[16,256]{1,0:T(8,128)}) custom-call(f32[256,3968]{1,0:T(8,128)} %all-gather.5.cloned.1.call-done.whole.refs_0_.refs_1_.refs_2_.refs_3_.refs_4_.refs_5_.range_grad, f32[256,3968]{1,0:T(8,128)} %all-gather.5.cloned.1.call-done.whole.refs_0_.refs_1_.refs_2_.refs_3_.refs_4_.refs_5_.range_grad, ...), custom_call_target="tpu_custom_call" | custom-call | tf_op jit(solution)/shard_map/right_products/pallas_call | solution.py:344
  215.4 2.1 collective-permute-start.37
  217.5 1.4 collective-permute-done.37
  219.0 1.1 dynamic-slice_add_fusion
  220.1 2.0 collective-permute-start.38
  223.1 11.0 %collective-permute-start.39 = (f32[112,256]{1,0:T(8,128)S(1)}, f32[112,256]{1,0:T(8,128)S(1)}, u32[]{:S(2)}, u32[]{:S(2)}) collective-permute-start(f32[112,256]{1,0:T(8,128)S(1)} %get-tuple-element.70), channel_id=1, source_target_pairs={{0,2},{1,3},{2,4},{3,5},{4,6},{5,7},{6,0},{7,1},{8,10},{9,11},{10,... | collective-permute-start | bytes 344072 | tf_op jit(solution)/shard_map/ppermute | solution.py:30
  235.8 2.7 collective-permute-done.39
  239.5 1.9 collective-permute-start.43
  241.4 8.6 %collective-permute-done.41 = f32[200,256]{1,0:T(8,128)S(1)} collective-permute-done((f32[200,256]{1,0:T(8,128)S(1)}, f32[200,256]{1,0:T(8,128)S(1)}, u32[]{:S(2)}, u32[]{:S(2)}) %collective-permute-start.41) | collective-permute-done | bytes 204832 | tf_op jit(solution)/shard_map/ppermute | solution.py:30
  250.1 2.4 collective-permute-start.44
  252.5 2.0 collective-permute-done.44
  255.5 4.0 %all-to-all-start = ((f32[16,16,256]{2,1,0:T(8,128)}), f32[16,16,256]{2,1,0:T(8,128)S(1)}, u32[]{:S(2)}, u32[]{:S(2)}) async-start(f32[16,16,256]{2,1,0:T(8,128)} %bitcast.6), calls=%async_computation | async-start | bytes 524288 | tf_op jit(solution)/shard_map/all_to_all | solution.py:558
  259.5 14.1 %factors.1 = (f32[256,256]{1,0:T(8,128)S(1)}, f32[256,256]{1,0:T(8,128)S(1)}, f32[8,128]{1,0:T(8,128)S(1)}) custom-call(f32[1600,256]{1,0:T(8,128)S(1)} %pad_maximum_fusion.right), custom_call_target="tpu_custom_call" | custom-call | tf_op jit(solution)/shard_map/factors/pallas_call | solution.py:469
  273.7 1.9 copy-done
  275.5 9.8 %last_update.1 = f32[384,3072]{1,0:T(8,128)} custom-call(f32[256,3072]{1,0:T(8,128)S(1)} %copy-done, f32[384,3072]{1,0:T(8,128)} %weight.3, f32[256,3968]{1,0:T(8,128)} %all-gather.5.cloned.1.call-done.whole.refs_0_.refs_1_.refs_2_.refs_3_.refs_4_.refs_5_.range_grad, f32[1600,256]{1,0:T(8,128)S(1)} %pad_maximum_fusion.right, f32[256,256]{1,0:T(8,128)S(1)} %bitcast.9, ...), custom_call_target="tpu_custom_call" | custom-call | tf_op jit(solution)/shard_map/last_update/pallas_call | solution.py:505
  (101 shorter events, 20.6 us)
Async XLA Ops:
  6.5 199.5 %all-gather.5.cloned.1.call-start = ((), (), s32[]{:S(2)}) async-start(), calls=%async_computation.2 | async-start | bytes 4317184 | tf_op jit(solution)/shard_map/all_gather | solution.py:542
  12.9 7.8 %collective-permute-start = (f32[768,512]{1,0:T(8,128)}, f32[768,512]{1,0:T(8,128)S(1)}, u32[]{:S(2)}, u32[]{:S(2)}) collective-permute-start(f32[768,512]{1,0:T(8,128)} %get-tuple-element.31), channel_id=1, source_target_pairs={{0,1},{1,0},{2,3},{3,2},{4,5},{5,4},{6,7},{7,6},{8,9},{9,8},{10,11... | collective-permute-start | bytes 4718600 | tf_op jit(solution)/shard_map/ppermute | solution.py:34
  22.4 1.1 copy-start.5
  23.6 12.3 %collective-permute-start.1 = (f32[192,512]{1,0:T(8,128)S(1)}, f32[192,512]{1,0:T(8,128)S(1)}, u32[]{:S(2)}, u32[]{:S(2)}) collective-permute-start(f32[192,512]{1,0:T(8,128)S(1)} %get-tuple-element.59), channel_id=1, source_target_pairs={{0,4},{1,5},{2,6},{3,7},{4,0},{5,1},{6,2},{7,3},{8,12},{9,13},{10,... | collective-permute-start | bytes 1179656 | tf_op jit(solution)/shard_map/ppermute | solution.py:30
  26.6 18.0 %collective-permute-start.3 = (f32[192,512]{1,0:T(8,128)S(1)}, f32[192,512]{1,0:T(8,128)S(1)}, u32[]{:S(2)}, u32[]{:S(2)}) collective-permute-start(f32[192,512]{1,0:T(8,128)S(1)} %get-tuple-element.60), channel_id=1, source_target_pairs={{0,6},{1,7},{2,0},{3,1},{4,2},{5,3},{6,4},{7,5},{8,14},{9,15},{10,... | collective-permute-start | bytes 1179656 | tf_op jit(solution)/shard_map/ppermute | solution.py:30
  27.4 17.3 %collective-permute-start.2 = (f32[192,512]{1,0:T(8,128)S(1)}, f32[192,512]{1,0:T(8,128)S(1)}, u32[]{:S(2)}, u32[]{:S(2)}) collective-permute-start(f32[192,512]{1,0:T(8,128)S(1)} %get-tuple-element.61), channel_id=1, source_target_pairs={{0,2},{1,3},{2,4},{3,5},{4,6},{5,7},{6,0},{7,1},{8,10},{9,11},{10,... | collective-permute-start | bytes 1179656 | tf_op jit(solution)/shard_map/ppermute | solution.py:30
  46.1 25.7 %copy-start.1 = (f32[16,128]{1,0:T(8,128)S(1)}, f32[16,128]{1,0:T(8,128)}, u32[]{:S(2)}) copy-start(f32[16,128]{1,0:T(8,128)} %get-tuple-element.32.sq_one) | copy-start | bytes 24580
  46.1 25.7 %copy-start.2 = (f32[16,128]{1,0:T(8,128)S(1)}, f32[16,128]{1,0:T(8,128)}, u32[]{:S(2)}) copy-start(f32[16,128]{1,0:T(8,128)} %get-tuple-element.33.sq_two) | copy-start | bytes 24580
  46.1 11.2 %collective-permute-start.4 = (f32[192,512]{1,0:T(8,128)S(1)}, f32[192,512]{1,0:T(8,128)S(1)}, u32[]{:S(2)}, u32[]{:S(2)}) collective-permute-start(f32[192,512]{1,0:T(8,128)S(1)} %get-tuple-element.56), channel_id=1, source_target_pairs={{0,2},{1,3},{2,4},{3,5},{4,6},{5,7},{6,0},{7,1},{8,10},{9,11},{10,... | collective-permute-start | bytes 1179656 | tf_op jit(solution)/shard_map/ppermute | solution.py:30
  47.5 19.6 %collective-permute-start.5 = (f32[192,512]{1,0:T(8,128)S(1)}, f32[192,512]{1,0:T(8,128)S(1)}, u32[]{:S(2)}, u32[]{:S(2)}) collective-permute-start(f32[192,512]{1,0:T(8,128)S(1)} %get-tuple-element.56), channel_id=1, source_target_pairs={{0,4},{1,5},{2,6},{3,7},{4,0},{5,1},{6,2},{7,3},{8,12},{9,13},{10,... | collective-permute-start | bytes 1179656 | tf_op jit(solution)/shard_map/ppermute | solution.py:30
  49.9 17.2 %collective-permute-start.6 = (f32[192,512]{1,0:T(8,128)S(1)}, f32[192,512]{1,0:T(8,128)S(1)}, u32[]{:S(2)}, u32[]{:S(2)}) collective-permute-start(f32[192,512]{1,0:T(8,128)S(1)} %get-tuple-element.56), channel_id=1, source_target_pairs={{0,6},{1,7},{2,0},{3,1},{4,2},{5,3},{6,4},{7,5},{8,14},{9,15},{10,... | collective-permute-start | bytes 1179656 | tf_op jit(solution)/shard_map/ppermute | solution.py:30
  67.2 4.6 %collective-permute-start.7 = (f32[768,512]{1,0:T(8,128)S(1)}, f32[768,512]{1,0:T(8,128)}, u32[]{:S(2)}, u32[]{:S(2)}) collective-permute-start(f32[768,512]{1,0:T(8,128)S(1)} %constant_dynamic-update-slice_fusion.8.own), channel_id=1, source_target_pairs={{0,1},{1,0},{2,3},{3,2},{4,5},{5,4},{6,7},{7,6},{8,9},{9,8},{10,11... | collective-permute-start | bytes 4718600 | tf_op jit(solution)/shard_map/ppermute | solution.py:34
  84.0 0.8 copy-start.3
  84.8 0.8 copy-start.4
  85.6 14.5 %collective-permute-start.8 = (f32[32,3968]{1,0:T(8,128)}, f32[32,3968]{1,0:T(8,128)S(1)}, u32[]{:S(2)}, u32[]{:S(2)}) collective-permute-start(f32[32,3968]{1,0:T(8,128)} %get-tuple-element.35), channel_id=1, source_target_pairs={{0,16},{8,24},{16,0},{24,8},{32,48},{40,56},{48,32},{56,40},{64,80... | collective-permute-start | bytes 1523720 | tf_op jit(solution)/shard_map/ppermute | solution.py:30
  88.5 23.2 %collective-permute-start.9 = (f32[32,3968]{1,0:T(8,128)}, f32[32,3968]{1,0:T(8,128)S(1)}, u32[]{:S(2)}, u32[]{:S(2)}) collective-permute-start(f32[32,3968]{1,0:T(8,128)} %get-tuple-element.36), channel_id=1, source_target_pairs={{0,8},{8,16},{16,24},{24,0},{32,40},{40,48},{48,56},{56,32},{64,72... | collective-permute-start | bytes 1523720 | tf_op jit(solution)/shard_map/ppermute | solution.py:30
  88.9 22.8 %collective-permute-start.10 = (f32[32,3968]{1,0:T(8,128)}, f32[32,3968]{1,0:T(8,128)S(1)}, u32[]{:S(2)}, u32[]{:S(2)}) collective-permute-start(f32[32,3968]{1,0:T(8,128)} %get-tuple-element.37), channel_id=1, source_target_pairs={{0,24},{8,0},{16,8},{24,16},{32,56},{40,32},{48,40},{56,48},{64,88... | collective-permute-start | bytes 1523720 | tf_op jit(solution)/shard_map/ppermute | solution.py:30
  91.2 25.0 %collective-permute-start.14 = (f32[32,3968]{1,0:T(8,128)}, f32[32,3968]{1,0:T(8,128)S(1)}, u32[]{:S(2)}, u32[]{:S(2)}) collective-permute-start(f32[32,3968]{1,0:T(8,128)} %copy-done.4), channel_id=1, source_target_pairs={{0,64},{8,72},{16,80},{24,88},{32,96},{40,104},{48,112},{56,120},{... | collective-permute-start | bytes 1523720 | tf_op jit(solution)/shard_map/ppermute | solution.py:30
  94.8 24.0 %collective-permute-start.15 = (f32[32,3968]{1,0:T(8,128)}, f32[32,3968]{1,0:T(8,128)S(1)}, u32[]{:S(2)}, u32[]{:S(2)}) collective-permute-start(f32[32,3968]{1,0:T(8,128)} %copy-done.3), channel_id=1, source_target_pairs={{0,32},{8,40},{16,48},{24,56},{32,64},{40,72},{48,80},{56,88},{64,... | collective-permute-start | bytes 1523720 | tf_op jit(solution)/shard_map/ppermute | solution.py:30
  100.1 18.6 %collective-permute-start.16 = (f32[32,3968]{1,0:T(8,128)S(1)}, f32[32,3968]{1,0:T(8,128)S(1)}, u32[]{:S(2)}, u32[]{:S(2)}) collective-permute-start(f32[32,3968]{1,0:T(8,128)S(1)} %get-tuple-element.41), channel_id=1, source_target_pairs={{0,96},{8,104},{16,112},{24,120},{32,0},{40,8},{48,16},{56,24},{64... | collective-permute-start | bytes 1523720 | tf_op jit(solution)/shard_map/ppermute | solution.py:30
  111.8 9.4 %collective-permute-start.11 = (f32[8,3968]{1,0:T(8,128)S(1)}, f32[8,3968]{1,0:T(8,128)S(1)}, u32[]{:S(2)}, u32[]{:S(2)}) collective-permute-start(f32[8,3968]{1,0:T(8,128)S(1)} %get-tuple-element.65), channel_id=1, source_target_pairs={{0,64},{8,72},{16,80},{24,88},{32,96},{40,104},{48,112},{56,120},{... | collective-permute-start | bytes 380936 | tf_op jit(solution)/shard_map/ppermute | solution.py:30
  115.8 7.5 %collective-permute-start.13 = (f32[8,3968]{1,0:T(8,128)S(1)}, f32[8,3968]{1,0:T(8,128)S(1)}, u32[]{:S(2)}, u32[]{:S(2)}) collective-permute-start(f32[8,3968]{1,0:T(8,128)S(1)} %get-tuple-element.66), channel_id=1, source_target_pairs={{0,96},{8,104},{16,112},{24,120},{32,0},{40,8},{48,16},{56,24},{64... | collective-permute-start | bytes 380936 | tf_op jit(solution)/shard_map/ppermute | solution.py:30
  116.2 7.1 %collective-permute-start.12 = (f32[8,3968]{1,0:T(8,128)S(1)}, f32[8,3968]{1,0:T(8,128)S(1)}, u32[]{:S(2)}, u32[]{:S(2)}) collective-permute-start(f32[8,3968]{1,0:T(8,128)S(1)} %get-tuple-element.67), channel_id=1, source_target_pairs={{0,32},{8,40},{16,48},{24,56},{32,64},{40,72},{48,80},{56,88},{64,... | collective-permute-start | bytes 380936 | tf_op jit(solution)/shard_map/ppermute | solution.py:30
  118.9 5.4 %collective-permute-start.17 = (f32[8,3968]{1,0:T(8,128)S(1)}, f32[8,3968]{1,0:T(8,128)S(1)}, u32[]{:S(2)}, u32[]{:S(2)}) collective-permute-start(f32[8,3968]{1,0:T(8,128)S(1)} %get-tuple-element.62), channel_id=1, source_target_pairs={{0,16},{8,24},{16,0},{24,8},{32,48},{40,56},{48,32},{56,40},{64,80... | collective-permute-start | bytes 380936 | tf_op jit(solution)/shard_map/ppermute | solution.py:30
  119.0 6.3 %collective-permute-start.19 = (f32[8,3968]{1,0:T(8,128)S(1)}, f32[8,3968]{1,0:T(8,128)S(1)}, u32[]{:S(2)}, u32[]{:S(2)}) collective-permute-start(f32[8,3968]{1,0:T(8,128)S(1)} %get-tuple-element.63), channel_id=1, source_target_pairs={{0,24},{8,0},{16,8},{24,16},{32,56},{40,32},{48,40},{56,48},{64,88... | collective-permute-start | bytes 380936 | tf_op jit(solution)/shard_map/ppermute | solution.py:30
  121.2 6.7 %collective-permute-start.18 = (f32[8,3968]{1,0:T(8,128)S(1)}, f32[8,3968]{1,0:T(8,128)S(1)}, u32[]{:S(2)}, u32[]{:S(2)}) collective-permute-start(f32[8,3968]{1,0:T(8,128)S(1)} %get-tuple-element.64), channel_id=1, source_target_pairs={{0,8},{8,16},{16,24},{24,0},{32,40},{40,48},{48,56},{56,32},{64,72... | collective-permute-start | bytes 380936 | tf_op jit(solution)/shard_map/ppermute | solution.py:30
  128.7 144.9 %all-gather.3.cloned.1.call-start = ((), (), s32[]{:S(2)}) async-start(), calls=%async_computation.1 | async-start | bytes 3342336 | tf_op jit(solution)/shard_map/all_gather | solution.py:549
  128.8 6.0 %collective-permute-start.20 = (f32[48,256]{1,0:T(8,128)S(1)}, f32[48,256]{1,0:T(8,128)S(1)}, u32[]{:S(2)}, u32[]{:S(2)}) collective-permute-start(f32[48,256]{1,0:T(8,128)S(1)} %pad_maximum_fusion.4), channel_id=1, source_target_pairs={{0,0},{1,16},{2,32},{3,48},{4,64},{5,80},{6,96},{7,112},{8,2},{9,1... | collective-permute-start | bytes 147464 | tf_op jit(solution)/shard_map/ppermute | solution.py:116
  134.8 11.0 %collective-permute-start.23 = (f32[48,256]{1,0:T(8,128)S(1)}, f32[48,256]{1,0:T(8,128)S(1)}, u32[]{:S(2)}, u32[]{:S(2)}) collective-permute-start(f32[48,256]{1,0:T(8,128)S(1)} %collective-permute-done.20), channel_id=1, source_target_pairs={{0,6},{1,7},{2,0},{3,1},{4,2},{5,3},{6,4},{7,5},{8,14},{9,15},{10,... | collective-permute-start | bytes 147464 | tf_op jit(solution)/shard_map/ppermute | solution.py:30
  140.7 5.0 %collective-permute-start.22 = (f32[48,256]{1,0:T(8,128)S(1)}, f32[48,256]{1,0:T(8,128)S(1)}, u32[]{:S(2)}, u32[]{:S(2)}) collective-permute-start(f32[48,256]{1,0:T(8,128)S(1)} %collective-permute-done.20), channel_id=1, source_target_pairs={{0,4},{1,5},{2,6},{3,7},{4,0},{5,1},{6,2},{7,3},{8,12},{9,13},{10,... | collective-permute-start | bytes 147464 | tf_op jit(solution)/shard_map/ppermute | solution.py:30
  141.3 4.5 %collective-permute-start.21 = (f32[48,256]{1,0:T(8,128)S(1)}, f32[48,256]{1,0:T(8,128)S(1)}, u32[]{:S(2)}, u32[]{:S(2)}) collective-permute-start(f32[48,256]{1,0:T(8,128)S(1)} %collective-permute-done.20), channel_id=1, source_target_pairs={{0,2},{1,3},{2,4},{3,5},{4,6},{5,7},{6,0},{7,1},{8,10},{9,11},{10,... | collective-permute-start | bytes 147464 | tf_op jit(solution)/shard_map/ppermute | solution.py:30
  145.8 3.7 %collective-permute-start.24 = (f32[192,256]{1,0:T(8,128)S(1)}, f32[192,256]{1,0:T(8,128)S(1)}, u32[]{:S(2)}, u32[]{:S(2)}) collective-permute-start(f32[192,256]{1,0:T(8,128)S(1)} %constant_dynamic-update-slice_fusion.4), channel_id=1, source_target_pairs={{0,1},{1,0},{2,3},{3,2},{4,5},{5,4},{6,7},{7,6},{8,9},{9,8},{10,11... | collective-permute-start | bytes 589832 | tf_op jit(solution)/shard_map/ppermute | solution.py:34
  155.3 14.6 %collective-permute-start.25 = (f32[32,3072]{1,0:T(8,128)S(1)}, f32[32,3072]{1,0:T(8,128)S(1)}, u32[]{:S(2)}, u32[]{:S(2)}) collective-permute-start(f32[32,3072]{1,0:T(8,128)S(1)} %get-tuple-element.43), channel_id=1, source_target_pairs={{0,16},{8,24},{16,0},{24,8},{32,48},{40,56},{48,32},{56,40},{64,80... | collective-permute-start | bytes 1179656 | tf_op jit(solution)/shard_map/ppermute | solution.py:30
  156.1 28.5 %collective-permute-start.26 = (f32[32,3072]{1,0:T(8,128)S(1)}, f32[32,3072]{1,0:T(8,128)S(1)}, u32[]{:S(2)}, u32[]{:S(2)}) collective-permute-start(f32[32,3072]{1,0:T(8,128)S(1)} %get-tuple-element.44), channel_id=1, source_target_pairs={{0,8},{8,16},{16,24},{24,0},{32,40},{40,48},{48,56},{56,32},{64,72... | collective-permute-start | bytes 1179656 | tf_op jit(solution)/shard_map/ppermute | solution.py:30
  157.6 27.1 %collective-permute-start.27 = (f32[32,3072]{1,0:T(8,128)S(1)}, f32[32,3072]{1,0:T(8,128)S(1)}, u32[]{:S(2)}, u32[]{:S(2)}) collective-permute-start(f32[32,3072]{1,0:T(8,128)S(1)} %get-tuple-element.45), channel_id=1, source_target_pairs={{0,24},{8,0},{16,8},{24,16},{32,56},{40,32},{48,40},{56,48},{64,88... | collective-permute-start | bytes 1179656 | tf_op jit(solution)/shard_map/ppermute | solution.py:30
  159.6 33.2 %collective-permute-start.31 = (f32[32,3072]{1,0:T(8,128)S(1)}, f32[32,3072]{1,0:T(8,128)S(1)}, u32[]{:S(2)}, u32[]{:S(2)}) collective-permute-start(f32[32,3072]{1,0:T(8,128)S(1)} %get-tuple-element.47), channel_id=1, source_target_pairs={{0,64},{8,72},{16,80},{24,88},{32,96},{40,104},{48,112},{56,120},{... | collective-permute-start | bytes 1179656 | tf_op jit(solution)/shard_map/ppermute | solution.py:30
  160.7 32.5 %collective-permute-start.32 = (f32[32,3072]{1,0:T(8,128)S(1)}, f32[32,3072]{1,0:T(8,128)S(1)}, u32[]{:S(2)}, u32[]{:S(2)}) collective-permute-start(f32[32,3072]{1,0:T(8,128)S(1)} %get-tuple-element.48), channel_id=1, source_target_pairs={{0,32},{8,40},{16,48},{24,56},{32,64},{40,72},{48,80},{56,88},{64,... | collective-permute-start | bytes 1179656 | tf_op jit(solution)/shard_map/ppermute | solution.py:30
  169.9 25.8 %collective-permute-start.33 = (f32[32,3072]{1,0:T(8,128)S(1)}, f32[32,3072]{1,0:T(8,128)S(1)}, u32[]{:S(2)}, u32[]{:S(2)}) collective-permute-start(f32[32,3072]{1,0:T(8,128)S(1)} %get-tuple-element.49), channel_id=1, source_target_pairs={{0,96},{8,104},{16,112},{24,120},{32,0},{40,8},{48,16},{56,24},{64... | collective-permute-start | bytes 1179656 | tf_op jit(solution)/shard_map/ppermute | solution.py:30
  184.8 14.5 %collective-permute-start.28 = (f32[8,3072]{1,0:T(8,128)S(1)}, f32[8,3072]{1,0:T(8,128)S(1)}, u32[]{:S(2)}, u32[]{:S(2)}) collective-permute-start(f32[8,3072]{1,0:T(8,128)S(1)} %get-tuple-element.71), channel_id=1, source_target_pairs={{0,64},{8,72},{16,80},{24,88},{32,96},{40,104},{48,112},{56,120},{... | collective-permute-start | bytes 294920 | tf_op jit(solution)/shard_map/ppermute | solution.py:30
  186.6 13.3 %collective-permute-start.30 = (f32[8,3072]{1,0:T(8,128)S(1)}, f32[8,3072]{1,0:T(8,128)S(1)}, u32[]{:S(2)}, u32[]{:S(2)}) collective-permute-start(f32[8,3072]{1,0:T(8,128)S(1)} %get-tuple-element.72), channel_id=1, source_target_pairs={{0,96},{8,104},{16,112},{24,120},{32,0},{40,8},{48,16},{56,24},{64... | collective-permute-start | bytes 294920 | tf_op jit(solution)/shard_map/ppermute | solution.py:30
  192.7 7.2 %collective-permute-start.29 = (f32[8,3072]{1,0:T(8,128)S(1)}, f32[8,3072]{1,0:T(8,128)S(1)}, u32[]{:S(2)}, u32[]{:S(2)}) collective-permute-start(f32[8,3072]{1,0:T(8,128)S(1)} %get-tuple-element.73), channel_id=1, source_target_pairs={{0,32},{8,40},{16,48},{24,56},{32,64},{40,72},{48,80},{56,88},{64,... | collective-permute-start | bytes 294920 | tf_op jit(solution)/shard_map/ppermute | solution.py:30
  195.8 5.1 %collective-permute-start.34 = (f32[8,3072]{1,0:T(8,128)S(1)}, f32[8,3072]{1,0:T(8,128)S(1)}, u32[]{:S(2)}, u32[]{:S(2)}) collective-permute-start(f32[8,3072]{1,0:T(8,128)S(1)} %get-tuple-element.74), channel_id=1, source_target_pairs={{0,16},{8,24},{16,0},{24,8},{32,48},{40,56},{48,32},{56,40},{64,80... | collective-permute-start | bytes 294920 | tf_op jit(solution)/shard_map/ppermute | solution.py:30
  198.4 4.0 %collective-permute-start.36 = (f32[8,3072]{1,0:T(8,128)S(1)}, f32[8,3072]{1,0:T(8,128)S(1)}, u32[]{:S(2)}, u32[]{:S(2)}) collective-permute-start(f32[8,3072]{1,0:T(8,128)S(1)} %get-tuple-element.75), channel_id=1, source_target_pairs={{0,24},{8,0},{16,8},{24,16},{32,56},{40,32},{48,40},{56,48},{64,88... | collective-permute-start | bytes 294920 | tf_op jit(solution)/shard_map/ppermute | solution.py:30
  199.3 5.9 %collective-permute-start.35 = (f32[8,3072]{1,0:T(8,128)S(1)}, f32[8,3072]{1,0:T(8,128)S(1)}, u32[]{:S(2)}, u32[]{:S(2)}) collective-permute-start(f32[8,3072]{1,0:T(8,128)S(1)} %get-tuple-element.76), channel_id=1, source_target_pairs={{0,8},{8,16},{16,24},{24,0},{32,40},{40,48},{48,56},{56,32},{64,72... | collective-permute-start | bytes 294920 | tf_op jit(solution)/shard_map/ppermute | solution.py:30
  215.4 3.6 %collective-permute-start.37 = (f32[448,256]{1,0:T(8,128)S(1)}, f32[448,256]{1,0:T(8,128)S(1)}, u32[]{:S(2)}, u32[]{:S(2)}) collective-permute-start(f32[448,256]{1,0:T(8,128)S(1)} %constant_dynamic-slice_fusion.3), channel_id=1, source_target_pairs={{0,1},{1,0},{2,3},{3,2},{4,5},{5,4},{6,7},{7,6},{8,9},{9,8},{10,11... | collective-permute-start | bytes 1376264 | tf_op jit(solution)/shard_map/ppermute | solution.py:34
  220.1 18.5 %copy-start.6 = (f32[16,256]{1,0:T(8,128)S(1)}, f32[16,256]{1,0:T(8,128)}, u32[]{:S(2)}) copy-start(f32[16,256]{1,0:T(8,128)} %get-tuple-element.51) | copy-start | bytes 49156
  220.1 15.7 %collective-permute-start.38 = (f32[112,256]{1,0:T(8,128)S(1)}, f32[112,256]{1,0:T(8,128)S(1)}, u32[]{:S(2)}, u32[]{:S(2)}) collective-permute-start(f32[112,256]{1,0:T(8,128)S(1)} %get-tuple-element.68), channel_id=1, source_target_pairs={{0,4},{1,5},{2,6},{3,7},{4,0},{5,1},{6,2},{7,3},{8,12},{9,13},{10,... | collective-permute-start | bytes 344072 | tf_op jit(solution)/shard_map/ppermute | solution.py:30
  222.2 13.7 %collective-permute-start.40 = (f32[112,256]{1,0:T(8,128)S(1)}, f32[112,256]{1,0:T(8,128)S(1)}, u32[]{:S(2)}, u32[]{:S(2)}) collective-permute-start(f32[112,256]{1,0:T(8,128)S(1)} %get-tuple-element.69), channel_id=1, source_target_pairs={{0,6},{1,7},{2,0},{3,1},{4,2},{5,3},{6,4},{7,5},{8,14},{9,15},{10,... | collective-permute-start | bytes 344072 | tf_op jit(solution)/shard_map/ppermute | solution.py:30
  223.1 15.4 %collective-permute-start.39 = (f32[112,256]{1,0:T(8,128)S(1)}, f32[112,256]{1,0:T(8,128)S(1)}, u32[]{:S(2)}, u32[]{:S(2)}) collective-permute-start(f32[112,256]{1,0:T(8,128)S(1)} %get-tuple-element.70), channel_id=1, source_target_pairs={{0,2},{1,3},{2,4},{3,5},{4,6},{5,7},{6,0},{7,1},{8,10},{9,11},{10,... | collective-permute-start | bytes 344072 | tf_op jit(solution)/shard_map/ppermute | solution.py:30
  238.7 11.3 %collective-permute-start.41 = (f32[200,256]{1,0:T(8,128)S(1)}, f32[200,256]{1,0:T(8,128)S(1)}, u32[]{:S(2)}, u32[]{:S(2)}) collective-permute-start(f32[200,256]{1,0:T(8,128)S(1)} %get-tuple-element.82), channel_id=1, source_target_pairs={{0,2},{1,3},{2,4},{3,5},{4,6},{5,7},{6,0},{7,1},{8,10},{9,11},{10,... | collective-permute-start | bytes 614408 | tf_op jit(solution)/shard_map/ppermute | solution.py:30
  238.7 11.3 %collective-permute-start.42 = (f32[200,256]{1,0:T(8,128)S(1)}, f32[200,256]{1,0:T(8,128)S(1)}, u32[]{:S(2)}, u32[]{:S(2)}) collective-permute-start(f32[200,256]{1,0:T(8,128)S(1)} %get-tuple-element.82), channel_id=1, source_target_pairs={{0,4},{1,5},{2,6},{3,7},{4,0},{5,1},{6,2},{7,3},{8,12},{9,13},{10,... | collective-permute-start | bytes 614408 | tf_op jit(solution)/shard_map/ppermute | solution.py:30
  239.5 10.5 %collective-permute-start.43 = (f32[200,256]{1,0:T(8,128)S(1)}, f32[200,256]{1,0:T(8,128)S(1)}, u32[]{:S(2)}, u32[]{:S(2)}) collective-permute-start(f32[200,256]{1,0:T(8,128)S(1)} %get-tuple-element.82), channel_id=1, source_target_pairs={{0,6},{1,7},{2,0},{3,1},{4,2},{5,3},{6,4},{7,5},{8,14},{9,15},{10,... | collective-permute-start | bytes 614408 | tf_op jit(solution)/shard_map/ppermute | solution.py:30
  250.1 4.4 %collective-permute-start.44 = (f32[800,256]{1,0:T(8,128)S(1)}, f32[800,256]{1,0:T(8,128)S(1)}, u32[]{:S(2)}, u32[]{:S(2)}) collective-permute-start(f32[800,256]{1,0:T(8,128)S(1)} %constant_dynamic-update-slice_fusion), channel_id=1, source_target_pairs={{0,1},{1,0},{2,3},{3,2},{4,5},{5,4},{6,7},{7,6},{8,9},{9,8},{10,11... | collective-permute-start | bytes 2457608 | tf_op jit(solution)/shard_map/ppermute | solution.py:34
  255.5 18.2 %all-to-all-start = ((f32[16,16,256]{2,1,0:T(8,128)}), f32[16,16,256]{2,1,0:T(8,128)S(1)}, u32[]{:S(2)}, u32[]{:S(2)}) async-start(f32[16,16,256]{2,1,0:T(8,128)} %bitcast.6), calls=%async_computation | async-start | bytes 524288 | tf_op jit(solution)/shard_map/all_to_all | solution.py:558
  273.6 1.9 copy-start
Sparse Core Ops, SparseCore 0:
  128.8 70.7 all-gather.4
  206.1 47.1 all-gather.2
where the time goes:
time: 298 us; the launch traced here: 292 us
  starting transfers between devices  101 us (34%)
  waiting for transfers between devices  99.7 us (33%)
  Pallas kernels  63.4 us (21%)
  between operations  14.1 us (5%)
  local copies, waits for them, and re-layouts  8.09 us (3%)
  other arithmetic  6.33 us (2%)
    ppermute x39, waiting for transfers between devices, send(): lax.ppermute(value, 'tensor' if kind == 'x' else 'dp', ring(kind, step))  89.8 us
    ppermute x39, starting transfers between devices, send(): lax.ppermute(value, 'tensor' if kind == 'x' else 'dp', ring(kind, step))  82.9 us
    pallas_call x1, Pallas kernels, factors(): call(functools.partial(factor_kernel, counts), [array(R, R), array(R, R),...  14.1 us
    pallas_call x2, Pallas kernels, sketches(): call(sketch_kernel, [array(count, 2 * R), array(16, 128)], vmem=VMEM_MOST...  12.7 us
    pallas_call x1, Pallas kernels, ranges(): call(functools.partial(ranges_kernel, tokens_all), [array(R // 8, total)]...  12.2 us
    ppermute x5, starting transfers between devices, swap_cores(): return lax.ppermute(value, 'tensor', [(i, i ^ 1) for i in range(8)])  10.1 us
    pallas_call x1, Pallas kernels, last_update(): call(last_kernel, array(count, columns), grid=(columns // TILE,), in_spec...  9.76 us
    pallas_call x1, Pallas kernels, right_products(): call(right_kernel, [array(896, R), array(16, R)], grid=(columns // TILE,)...  8.28 us
  transfers between devices with their start and end apart: 48, of which 26 were waited for; matrix products, arithmetic and copies ran while one was open for 2% of the time, Pallas kernels for 12%

commit v1 on v0

--- a/solution.py
+++ b/solution.py
@@ -132,6 +132,16 @@
     )
 
 
+def stacked_product(left, right, dims):
+    (lh, ll), (rh, rl) = left, right
+    count = lh.shape[0]
+    dot = functools.partial(
+        lax.dot_general, dimension_numbers=(dims, ((), ())), preferred_element_type=jnp.float32
+    )
+    both = dot(jnp.concatenate([lh, ll]), rh)
+    return both[:count] + (both[count:] + dot(lh, rl))
+
+
 def call(kernel, out_shape, vmem=VMEM_LIMIT, **options):
     return pl.pallas_call(
         kernel,
@@ -154,9 +164,11 @@
         def _():
             total[...] = jnp.zeros_like(total)
 
-        out[:, i * R : i * R + R] = jnp.dot(
-            value[...], sketch[...], preferred_element_type=jnp.float32
-        )
+        half = value.shape[0] // 2
+        for at in (0, half):
+            out[at : at + half, i * R : i * R + R] = jnp.dot(
+                value[at : at + half, :], sketch[...], preferred_element_type=jnp.float32
+            )
         count, columns = value.shape
         for low in range(0, columns, 256):
             sums = jnp.zeros((16, 256), jnp.float32)
@@ -316,54 +328,77 @@
 
 
 def right_kernel(whole, *refs):
-    extra, (weight, left, sums, both) = refs[:6], refs[6:]
+    extra, (weight, left, sums, cores, both) = refs[:7], refs[7:]
 
     @pl.when(pl.program_id(0) == 0)
     def _():
         sums[...] = jnp.zeros_like(sums)
         both[...] = jnp.zeros_like(both)
-        blocks = [jnp.concatenate([extra[i][...], extra[i + 1][...]], axis=1) for i in (0, 2, 4)]
+        cores[...] = extra[0][...].T[:64]
+        blocks = [jnp.concatenate([extra[i][...], extra[i + 1][...]], axis=1) for i in (1, 3, 5)]
         pieces = split(jnp.concatenate(blocks))
         gram = product(pieces, pieces, ((0,), (0,)))
         for i in range(8):
-            sums[i * 112 + 80 : i * 112 + 112, :] = gram[i * 32 : i * 32 + 32]
+            sums[i * 120 + 80 : i * 120 + 112, :] = gram[i * 32 : i * 32 + 32]
+            sums[i * 120 + 112 : i * 120 + 120, :128] = extra[0][:8, :]
 
     ranges = split(whole[...])
-    right = product(split(weight[...]), ranges, LAST)
-    gram = product(ranges, ranges, LAST)
+    lines = [split(weight[...]), ranges, split(left[...])]
+    lines = [jnp.concatenate([line[i] for line in lines]) for i in range(2)]
+    total = stacked_product(lines, ranges, LAST)
+    count = weight.shape[0]
     for i in range(8):
-        at = i * 112
-        sums[at : at + 48, :] += right[i * 48 : i * 48 + 48]
-        sums[at + 48 : at + 80, :] += gram[i * 32 : i * 32 + 32]
-    both[...] += product(split(left[...]), ranges, LAST)
+        at, gram = i * 120, count + i * 32
+        sums[at : at + 48, :] += total[i * 48 : i * 48 + 48]
+        sums[at + 48 : at + 80, :] += total[gram : gram + 32]
+    both[...] += total[count + R :]
 
 
 def right_products(gathered, weight, left):
     count, columns = weight.shape
-    extra = lambda i: pl.BlockSpec((R, 128), lambda j: (0, columns // 128 + 1 + i))
+    extra = lambda i: pl.BlockSpec((R, 128), lambda j: (0, columns // 128 + i))
+    fixed = lambda shape: pl.BlockSpec(shape, lambda j: (0, 0))
     return call(
         right_kernel,
-        [array(896, R), array(16, R)],
+        [array(960, R), array(64, R), array(16, R)],
         grid=(columns // TILE,),
         in_specs=[pl.BlockSpec((R, TILE), lambda j: (0, j))]
-        + [extra(i) for i in range(6)]
+        + [extra(i) for i in range(7)]
         + [
             pl.BlockSpec((count, TILE), lambda j: (0, j)),
             pl.BlockSpec((16, TILE), lambda j: (0, j)),
         ],
-        out_specs=[
-            pl.BlockSpec((896, R), lambda j: (0, 0)),
-            pl.BlockSpec((16, R), lambda j: (0, 0)),
-        ],
+        out_specs=[fixed((960, R)), fixed((64, R)), fixed((16, R))],
         vmem=VMEM_MOST,
         name="right_products",
-    )(*[gathered] * 7, weight, left)
+    )(*[gathered] * 8, weight, left)
+
+
+def combine_kernel(counts, sums, cores, both, out, scale):
+    damp_grad = DAMPING * sums[112:113, 64:65] / counts[0]
+    damp_act = DAMPING * sums[112:113, 65:66] / counts[1]
+    scale[...] = jnp.broadcast_to(1.0 / (damp_act * damp_grad), (8, 128))
+    out[0:48, :] = sums[0:48, :]
+    out[48:80, :] = damp_grad * cores[0:32, :] + sums[48:80, :]
+    out[80:112, :] = damp_act * cores[32:64, :] + sums[80:112, :]
+    out[112:128, :] = both[...]
+
+
+def combine(sums, cores, both, counts):
+    whole = pl.BlockSpec(memory_space=pltpu.VMEM)
+    return call(
+        functools.partial(combine_kernel, counts),
+        [array(128, R), array(8, 128)],
+        in_specs=[whole] * 3,
+        out_specs=[whole] * 2,
+        name="combine",
+    )(sums, cores, both)
 
 
 def pack_kernel(right, out):
-    total = right[184:200, :]
+    total = right[112:128, :]
     for i in range(1, 8):
-        total += right[i * 200 + 184 : i * 200 + 200, :]
+        total += right[i * 128 + 112 : i * 128 + 128, :]
     for d in range(16):
         out[16 * d : 16 * d + 16, :] = total
 
@@ -443,34 +478,26 @@
                 w[high:, :] -= exact(line[:, high:R], line, ((0,), (0,)))
 
 
-def factor_kernel(counts, right, inverse_act, inverse_grad, scale, *work):
-    trace_grad, trace_act = jnp.zeros((1, 1)), jnp.zeros((1, 1))
-    for i in range(8):
-        at = i * 200 + 176
-        trace_grad += right[at : at + 1, 64:65]
-        trace_act += right[at : at + 1, 65:66]
-    damp_grad = DAMPING * trace_grad / counts[0]
-    damp_act = DAMPING * trace_act / counts[1]
-    scale[...] = jnp.broadcast_to(1.0 / (damp_act * damp_grad), (8, 128))
+def factor_kernel(right, inverse_act, inverse_grad, *work):
     row = lax.broadcasted_iota(jnp.int32, (R, R), 0)
     column = lax.broadcasted_iota(jnp.int32, (R, R), 1)
     identity = jnp.where(row == column, 1.0, 0.0)
     for w in work:
         w[:, R:] = identity
     for i in range(8):
-        at, here = slice(i * 32, i * 32 + 32), i * 200
-        work[0][at, :R] = damp_act * right[here + 144 : here + 176, :] + right[here + 80 : here + 112, :]
-        work[1][at, :R] = damp_grad * right[here + 112 : here + 144, :] + right[here + 48 : here + 80, :]
+        at, here = slice(i * 32, i * 32 + 32), i * 128
+        work[0][at, :R] = right[here + 80 : here + 112, :]
+        work[1][at, :R] = right[here + 48 : here + 80, :]
     lower_inverses(work, (inverse_act, inverse_grad))
 
 
-def factors(right, counts):
+def factors(right):
     whole = pl.BlockSpec(memory_space=pltpu.VMEM)
     return call(
-        functools.partial(factor_kernel, counts),
-        [array(R, R), array(R, R), array(8, 128)],
+        factor_kernel,
+        [array(R, R), array(R, R)],
         in_specs=[whole],
-        out_specs=[whole] * 3,
+        out_specs=[whole] * 2,
         scratch_shapes=[pltpu.VMEM((R, 2 * R), jnp.float32)] * 2,
         name="factors",
     )(right)
@@ -488,7 +515,7 @@
     @pl.when(pl.program_id(0) == 0)
     def _():
         for i in range(8):
-            sums[i * 48 : i * 48 + 48, :] = right[i * 200 : i * 200 + 48, :]
+            sums[i * 48 : i * 48 + 48, :] = right[i * 128 : i * 128 + 48, :]
         solved = applied(rows_act[...], inverse_act[...])
         pieces[0][...], pieces[1][...] = split(solved)
         rest = sums[...] - product(split(solved), split(both[...]), INNER)
@@ -528,7 +555,6 @@
     columns = weight_grad.shape[1]
     core_id = lax.axis_index("tensor") % 2
     places = jnp.stack([tensor_chunk(), core_id, place("y"), place("z")]).astype(jnp.int32)
-    width = R // 8
 
     part, sq_one = sketches(1 - core_id, grads_out, acts, sketch_out, sketch_in)
     other = swap_cores(part)
@@ -548,17 +574,13 @@
     piece = scatter_dp(left_products(places, rows_act, weight_grad))
     left_sums = lax.all_gather(piece, "dp", axis=0, tiled=True)
 
-    part, both = right_products(gathered, weight_grad, piece)
-    part = scatter_tensor(part)
-    extra = gathered[:, columns:at]
-    cores = extra[:, : 2 * width].T
-    rest = jnp.pad(extra[:8], ((0, 0), (0, R - 128)))
-    part = jnp.concatenate([part, cores, rest, both])
+    counts = (float(tokens_all * FF), float(tokens_all * D))
+    part, cores, both = right_products(gathered, weight_grad, piece)
+    part, scale = combine(scatter_tensor(part), cores, both, counts)
     right = gather_tensor(part)
     both = lax.all_to_all(pack(right), "dp", 0, 0, tiled=True)
 
-    counts = (float(tokens_all * FF), float(tokens_all * D))
-    inverse_act, inverse_grad, scale = factors(right, counts)
+    inverse_act, inverse_grad = factors(right)
     return last_update(
         left_sums, weight_grad, gathered, right, both, rows_act, inverse_act, inverse_grad, scale
     )

time: 298 us -> 294 us (0.987)
    pallas_call x2 -> x3, Pallas kernels: 22.4 us -> 21.9 us  [the longest x1 14 us: factors(): call(factor_kernel, [array(R, R), array(R, R)], in_specs=[whole], out_spe...]
  transfers between devices with their start and end apart: 48 -> 48, of which waited for: 26 -> 30; matrix products, arithmetic and copies ran while one was open for 2% -> 1% of each run, Pallas kernels for 12% -> 12%
where the time goes in v1:
time: 294 us; the launch traced here: 290 us
  starting transfers between devices  102 us (35%)
  waiting for transfers between devices  99.7 us (34%)
  Pallas kernels  61.8 us (21%)
  between operations  14.1 us (5%)
  local copies, waits for them, and re-layouts  6.97 us (2%)
  other arithmetic  6.18 us (2%)
    ppermute x39, waiting for transfers between devices, send(): lax.ppermute(value, 'tensor' if kind == 'x' else 'dp', ring(kind, step))  90.2 us
    ppermute x39, starting transfers between devices, send(): lax.ppermute(value, 'tensor' if kind == 'x' else 'dp', ring(kind, step))  80.2 us
    pallas_call x1, Pallas kernels, factors(): call(factor_kernel, [array(R, R), array(R, R)], in_specs=[whole], out_spe...  14 us
    pallas_call x1, Pallas kernels, ranges(): call(functools.partial(ranges_kernel, tokens_all), [array(R // 8, total)]...  12.2 us
    ppermute x5, starting transfers between devices, swap_cores(): return lax.ppermute(value, 'tensor', [(i, i ^ 1) for i in range(8)])  12.2 us
    pallas_call x2, Pallas kernels, sketches(): call(sketch_kernel, [array(count, 2 * R), array(16, 128)], vmem=VMEM_MOST...  11.6 us
    pallas_call x1, Pallas kernels, last_update(): call(last_kernel, array(count, columns), grid=(columns // TILE,), in_spec...  9.75 us
    pallas_call x1, Pallas kernels, right_products(): call(right_kernel, [array(960, R), array(64, R), array(16, R)], grid=(col...  7.71 us
  transfers between devices with their start and end apart: 48, of which 30 were waited for; matrix products, arithmetic and copies ran while one was open for 1% of the time, Pallas kernels for 12%

profile of v1, /device:TPU:1, one launch (start us, length us, event | category | flops | bytes accessed | tf_op | source)
XLA Modules:
  0.0 290.3 jit_solution(18274173733445024211)
XLA Ops:
  6.5 5.8 %sketches.3 = (f32[768,512]{1,0:T(8,128)}, f32[16,128]{1,0:T(8,128)}) custom-call(s32[1]{0:T(128)} %bitcast.4.core, bf16[1536,3072]{1,0:T(8,128)(2,1)} %grads.5, bf16[1536,768]{1,0:T(8,128)(2,1)} %acts.5, bf16[3072,256]{1,0:T(8,128)(2,1)} %sketch_out.3, bf16[768,256]{1,0:T(8,128)(2,1)} %sketch_in.3), custom_call_target="tpu_custom_call" | custom-call | tf_op jit(solution)/shard_map/sketches/pallas_call | solution.py:209
  12.4 1.4 collective-permute-start
  13.8 5.8 %sketches.2 = (f32[768,512]{1,0:T(8,128)}, f32[16,128]{1,0:T(8,128)}) custom-call(s32[1]{0:T(128)} %bitcast.1.core, bf16[1536,3072]{1,0:T(8,128)(2,1)} %grads.5, bf16[1536,768]{1,0:T(8,128)(2,1)} %acts.5, bf16[3072,256]{1,0:T(8,128)(2,1)} %sketch_out.3, bf16[768,256]{1,0:T(8,128)(2,1)} %sketch_in.3), custom_call_target="tpu_custom_call" | custom-call | tf_op jit(solution)/shard_map/sketches/pallas_call | solution.py:209
  19.6 1.8 add.318
  21.4 2.9 %collective-permute-start.1 = (f32[192,512]{1,0:T(8,128)S(1)}, f32[192,512]{1,0:T(8,128)S(1)}, u32[]{:S(2)}, u32[]{:S(2)}) collective-permute-start(f32[192,512]{1,0:T(8,128)S(1)} %get-tuple-element.61), channel_id=1, source_target_pairs={{0,4},{1,5},{2,6},{3,7},{4,0},{5,1},{6,2},{7,3},{8,12},{9,13},{10,... | collective-permute-start | bytes 1179656 | tf_op jit(solution)/shard_map/ppermute | solution.py:30
  25.8 7.9 %collective-permute-done.1 = f32[192,512]{1,0:T(8,128)S(1)} collective-permute-done((f32[192,512]{1,0:T(8,128)S(1)}, f32[192,512]{1,0:T(8,128)S(1)}, u32[]{:S(2)}, u32[]{:S(2)}) %collective-permute-start.1) | collective-permute-done | bytes 393248 | tf_op jit(solution)/shard_map/ppermute | solution.py:30
  33.8 8.7 %collective-permute-done.3 = f32[192,512]{1,0:T(8,128)S(1)} collective-permute-done((f32[192,512]{1,0:T(8,128)S(1)}, f32[192,512]{1,0:T(8,128)S(1)}, u32[]{:S(2)}, u32[]{:S(2)}) %collective-permute-start.3) | collective-permute-done | bytes 393248 | tf_op jit(solution)/shard_map/ppermute | solution.py:30
  44.3 1.1 constant_dynamic-update-slice_fusion.11
  45.5 1.5 collective-permute-start.4
  47.0 2.3 collective-permute-start.5
  49.9 6.8 %collective-permute-done.4 = f32[192,512]{1,0:T(8,128)S(1)} collective-permute-done((f32[192,512]{1,0:T(8,128)S(1)}, f32[192,512]{1,0:T(8,128)S(1)}, u32[]{:S(2)}, u32[]{:S(2)}) %collective-permute-start.4) | collective-permute-done | bytes 393248 | tf_op jit(solution)/shard_map/ppermute | solution.py:30
  56.7 9.9 %collective-permute-done.5 = f32[192,512]{1,0:T(8,128)S(1)} collective-permute-done((f32[192,512]{1,0:T(8,128)S(1)}, f32[192,512]{1,0:T(8,128)S(1)}, u32[]{:S(2)}, u32[]{:S(2)}) %collective-permute-start.5) | collective-permute-done | bytes 393248 | tf_op jit(solution)/shard_map/ppermute | solution.py:30
  66.6 1.4 collective-permute-start.7
  68.1 3.1 %collective-permute-done.7.other = f32[768,512]{1,0:T(8,128)} collective-permute-done((f32[768,512]{1,0:T(8,128)S(1)}, f32[768,512]{1,0:T(8,128)}, u32[]{:S(2)}, u32[]{:S(2)}) %collective-permute-start.7) | collective-permute-done | bytes 1572896 | tf_op jit(solution)/shard_map/ppermute | solution.py:34
  71.2 12.2 %ranges.1 = (f32[32,3968]{1,0:T(8,128)S(1)}, f32[32,3968]{1,0:T(8,128)}, f32[32,3968]{1,0:T(8,128)}, f32[32,3968]{1,0:T(8,128)}, f32[32,3968]{1,0:T(8,128)S(1)},...) custom-call(s32[4]{0:T(128)S(1)} %pad_add_fusion.places, ...), custom_call_target="tpu_custom_call" | custom-call | tf_op jit(solution)/shard_map/ranges/pallas_call | solution.py:291
  85.0 2.9 %collective-permute-start.8 = (f32[32,3968]{1,0:T(8,128)}, f32[32,3968]{1,0:T(8,128)S(1)}, u32[]{:S(2)}, u32[]{:S(2)}) collective-permute-start(f32[32,3968]{1,0:T(8,128)} %get-tuple-element.37), channel_id=1, source_target_pairs={{0,16},{8,24},{16,0},{24,8},{32,48},{40,56},{48,32},{56,40},{64,80... | collective-permute-start | bytes 1523720 | tf_op jit(solution)/shard_map/ppermute | solution.py:30
  88.4 2.3 collective-permute-start.10
  90.6 3.6 %collective-permute-start.14 = (f32[32,3968]{1,0:T(8,128)}, f32[32,3968]{1,0:T(8,128)S(1)}, u32[]{:S(2)}, u32[]{:S(2)}) collective-permute-start(f32[32,3968]{1,0:T(8,128)} %copy-done.6), channel_id=1, source_target_pairs={{0,64},{8,72},{16,80},{24,88},{32,96},{40,104},{48,112},{56,120},{... | collective-permute-start | bytes 1523720 | tf_op jit(solution)/shard_map/ppermute | solution.py:30
  95.0 4.6 %collective-permute-done.8 = f32[32,3968]{1,0:T(8,128)S(1)} collective-permute-done((f32[32,3968]{1,0:T(8,128)}, f32[32,3968]{1,0:T(8,128)S(1)}, u32[]{:S(2)}, u32[]{:S(2)}) %collective-permute-start.8) | collective-permute-done | bytes 507936 | tf_op jit(solution)/shard_map/ppermute | solution.py:30
  99.6 3.8 %collective-permute-start.16 = (f32[32,3968]{1,0:T(8,128)S(1)}, f32[32,3968]{1,0:T(8,128)S(1)}, u32[]{:S(2)}, u32[]{:S(2)}) collective-permute-start(f32[32,3968]{1,0:T(8,128)S(1)} %get-tuple-element.43), channel_id=1, source_target_pairs={{0,96},{8,104},{16,112},{24,120},{32,0},{40,8},{48,16},{56,24},{64... | collective-permute-start | bytes 1523720 | tf_op jit(solution)/shard_map/ppermute | solution.py:30
  103.4 7.7 %collective-permute-done.9 = f32[32,3968]{1,0:T(8,128)S(1)} collective-permute-done((f32[32,3968]{1,0:T(8,128)}, f32[32,3968]{1,0:T(8,128)S(1)}, u32[]{:S(2)}, u32[]{:S(2)}) %collective-permute-start.9) | collective-permute-done | bytes 507936 | tf_op jit(solution)/shard_map/ppermute | solution.py:30
  111.3 3.7 %collective-permute-start.11 = (f32[8,3968]{1,0:T(8,128)S(1)}, f32[8,3968]{1,0:T(8,128)S(1)}, u32[]{:S(2)}, u32[]{:S(2)}) collective-permute-start(f32[8,3968]{1,0:T(8,128)S(1)} %get-tuple-element.69), channel_id=1, source_target_pairs={{0,64},{8,72},{16,80},{24,88},{32,96},{40,104},{48,112},{56,120},{... | collective-permute-start | bytes 380936 | tf_op jit(solution)/shard_map/ppermute | solution.py:30
  116.7 1.8 collective-permute-done.15
  118.8 1.9 collective-permute-start.19
  120.6 1.9 collective-permute-done.13
  122.5 1.5 collective-permute-done.17
  124.8 2.4 collective-permute-done.18
  128.0 3.9 %collective-permute-start.20 = (f32[48,256]{1,0:T(8,128)S(1)}, f32[48,256]{1,0:T(8,128)S(1)}, u32[]{:S(2)}, u32[]{:S(2)}) collective-permute-start(f32[48,256]{1,0:T(8,128)S(1)} %pad_maximum_fusion.4), channel_id=1, source_target_pairs={{0,0},{1,16},{2,32},{3,48},{4,64},{5,80},{6,96},{7,112},{8,2},{9,1... | collective-permute-start | bytes 147464 | tf_op jit(solution)/shard_map/ppermute | solution.py:116
  132.0 2.2 collective-permute-done.20
  134.2 5.8 %collective-permute-start.23 = (f32[48,256]{1,0:T(8,128)S(1)}, f32[48,256]{1,0:T(8,128)S(1)}, u32[]{:S(2)}, u32[]{:S(2)}) collective-permute-start(f32[48,256]{1,0:T(8,128)S(1)} %collective-permute-done.20), channel_id=1, source_target_pairs={{0,6},{1,7},{2,0},{3,1},{4,2},{5,3},{6,4},{7,5},{8,14},{9,15},{10,... | collective-permute-start | bytes 147464 | tf_op jit(solution)/shard_map/ppermute | solution.py:30
  140.8 3.9 %collective-permute-done.21 = f32[48,256]{1,0:T(8,128)S(1)} collective-permute-done((f32[48,256]{1,0:T(8,128)S(1)}, f32[48,256]{1,0:T(8,128)S(1)}, u32[]{:S(2)}, u32[]{:S(2)}) %collective-permute-start.21) | collective-permute-done | bytes 49184 | tf_op jit(solution)/shard_map/ppermute | solution.py:30
  144.7 2.8 collective-permute-start.24
  147.6 1.1 collective-permute-done.24
  148.7 5.6 %left_products.1 = (f32[32,3072]{1,0:T(8,128)S(1)}, f32[32,3072]{1,0:T(8,128)S(1)}, f32[32,3072]{1,0:T(8,128)S(1)}, f32[32,3072]{1,0:T(8,128)S(1)}, f32[32,3072]...) custom-call(s32[4]{0:T(128)S(1)} %pad_add_fusion.places, ...), custom_call_target="tpu_custom_call" | custom-call | tf_op jit(solution)/shard_map/left_products/pallas_call | solution.py:325
  154.7 2.2 collective-permute-start.26
  156.9 1.9 collective-permute-start.27
  158.8 1.5 collective-permute-start.31
  160.3 2.4 collective-permute-start.32
  162.7 6.6 %collective-permute-done.25 = f32[32,3072]{1,0:T(8,128)S(1)} collective-permute-done((f32[32,3072]{1,0:T(8,128)S(1)}, f32[32,3072]{1,0:T(8,128)S(1)}, u32[]{:S(2)}, u32[]{:S(2)}) %collective-permute-start.25) | collective-permute-done | bytes 393248 | tf_op jit(solution)/shard_map/ppermute | solution.py:30
  169.3 7.4 %collective-permute-start.33 = (f32[32,3072]{1,0:T(8,128)S(1)}, f32[32,3072]{1,0:T(8,128)S(1)}, u32[]{:S(2)}, u32[]{:S(2)}) collective-permute-start(f32[32,3072]{1,0:T(8,128)S(1)} %get-tuple-element.51), channel_id=1, source_target_pairs={{0,96},{8,104},{16,112},{24,120},{32,0},{40,8},{48,16},{56,24},{64... | collective-permute-start | bytes 1179656 | tf_op jit(solution)/shard_map/ppermute | solution.py:30
  176.7 7.1 %collective-permute-done.26 = f32[32,3072]{1,0:T(8,128)S(1)} collective-permute-done((f32[32,3072]{1,0:T(8,128)S(1)}, f32[32,3072]{1,0:T(8,128)S(1)}, u32[]{:S(2)}, u32[]{:S(2)}) %collective-permute-start.26) | collective-permute-done | bytes 393248 | tf_op jit(solution)/shard_map/ppermute | solution.py:30
  184.0 2.2 collective-permute-start.28
  186.2 6.1 %collective-permute-start.30 = (f32[8,3072]{1,0:T(8,128)S(1)}, f32[8,3072]{1,0:T(8,128)S(1)}, u32[]{:S(2)}, u32[]{:S(2)}) collective-permute-start(f32[8,3072]{1,0:T(8,128)S(1)} %get-tuple-element.76), channel_id=1, source_target_pairs={{0,96},{8,104},{16,112},{24,120},{32,0},{40,8},{48,16},{56,24},{64... | collective-permute-start | bytes 294920 | tf_op jit(solution)/shard_map/ppermute | solution.py:30
  192.8 1.6 collective-permute-done.33
  194.5 2.6 collective-permute-start.34
  199.6 1.3 collective-permute-done.36
  200.9 2.7 collective-permute-done.35
  204.3 7.7 %right_products.1 = (f32[960,256]{1,0:T(8,128)}, f32[64,256]{1,0:T(8,128)}, f32[16,256]{1,0:T(8,128)}) custom-call(f32[256,3968]{1,0:T(8,128)} %all-gather.5.cloned.1.call-done.whole.refs_0_.refs_1_.refs_2_.refs_3_.refs_4_.refs_5_.refs_6_.range_grad, ...), custom_call_target="tpu_custom_call" | custom-call | tf_op jit(solution)/shard_map/right_products/pallas_call | solution.py:361
  212.0 1.1 constant_dynamic-slice_fusion.3
  213.1 3.9 %collective-permute-start.37 = (f32[480,256]{1,0:T(8,128)S(1)}, f32[480,256]{1,0:T(8,128)S(1)}, u32[]{:S(2)}, u32[]{:S(2)}) collective-permute-start(f32[480,256]{1,0:T(8,128)S(1)} %constant_dynamic-slice_fusion.3), channel_id=1, source_target_pairs={{0,1},{1,0},{2,3},{3,2},{4,5},{5,4},{6,7},{7,6},{8,9},{9,8},{10,11... | collective-permute-start | bytes 1474568 | tf_op jit(solution)/shard_map/ppermute | solution.py:34
  217.0 1.5 collective-permute-done.37
  218.5 1.1 dynamic-slice_add_fusion
  221.9 3.9 %collective-permute-done.38 = f32[120,256]{1,0:T(8,128)S(1)} collective-permute-done((f32[120,256]{1,0:T(8,128)S(1)}, f32[120,256]{1,0:T(8,128)S(1)}, u32[]{:S(2)}, u32[]{:S(2)}) %collective-permute-start.38) | collective-permute-done | bytes 122912 | tf_op jit(solution)/shard_map/ppermute | solution.py:30
  226.2 2.4 collective-permute-done.39
  228.9 10.2 %collective-permute-start.41 = (f32[128,256]{1,0:T(8,128)S(1)}, f32[128,256]{1,0:T(8,128)S(1)}, u32[]{:S(2)}, u32[]{:S(2)}) collective-permute-start(f32[128,256]{1,0:T(8,128)S(1)} %get-tuple-element.55), channel_id=1, source_target_pairs={{0,2},{1,3},{2,4},{3,5},{4,6},{5,7},{6,0},{7,1},{8,10},{9,11},{10,... | collective-permute-start | bytes 393224 | tf_op jit(solution)/shard_map/ppermute | solution.py:30
  239.2 2.6 collective-permute-start.43
  241.9 2.7 collective-permute-done.41
  244.6 2.6 collective-permute-done.42
  247.2 2.7 collective-permute-start.44
  249.9 1.5 collective-permute-done.44
  252.3 5.2 %all-to-all-start = ((f32[16,16,256]{2,1,0:T(8,128)}), f32[16,16,256]{2,1,0:T(8,128)S(1)}, u32[]{:S(2)}, u32[]{:S(2)}) async-start(f32[16,16,256]{2,1,0:T(8,128)} %bitcast.5), calls=%async_computation | async-start | bytes 524288 | tf_op jit(solution)/shard_map/all_to_all | solution.py:581
  257.6 14.0 %factors.1 = (f32[256,256]{1,0:T(8,128)S(1)}, f32[256,256]{1,0:T(8,128)S(1)}) custom-call(f32[1024,256]{1,0:T(8,128)S(1)} %pad_maximum_fusion.right), custom_call_target="tpu_custom_call" | custom-call | tf_op jit(solution)/shard_map/factors/pallas_call | solution.py:496
  271.6 1.9 copy-done
  273.5 9.8 %last_update.1 = f32[384,3072]{1,0:T(8,128)} custom-call(f32[256,3072]{1,0:T(8,128)S(1)} %copy-done, f32[384,3072]{1,0:T(8,128)} %weight.3, f32[256,3968]{1,0:T(8,128)} %all-gather.5.cloned.1.call-done.whole.refs_0_.refs_1_.refs_2_.refs_3_.refs_4_.refs_5_.refs_6_.range_grad, f32[1024,256]{1,0:T(8,128)S(1)} %pad_maximum_fusion.right, f32[256,256]{1,0:T(8,128)S(1)} %bitcast.7, ...), custom_call_target="tpu_custom_call" | custom-call | tf_op jit(solution)/shard_map/last_update/pallas_call | solution.py:532
  (107 shorter events, 20.0 us)
Async XLA Ops:
  6.5 197.8 %all-gather.5.cloned.1.call-start = ((), (), s32[]{:S(2)}) async-start(), calls=%async_computation.2 | async-start | bytes 4317184 | tf_op jit(solution)/shard_map/all_gather | solution.py:568
  12.4 7.2 %collective-permute-start = (f32[768,512]{1,0:T(8,128)}, f32[768,512]{1,0:T(8,128)S(1)}, u32[]{:S(2)}, u32[]{:S(2)}) collective-permute-start(f32[768,512]{1,0:T(8,128)} %get-tuple-element.33), channel_id=1, source_target_pairs={{0,1},{1,0},{2,3},{3,2},{4,5},{5,4},{6,7},{7,6},{8,9},{9,8},{10,11... | collective-permute-start | bytes 4718600 | tf_op jit(solution)/shard_map/ppermute | solution.py:34
  21.4 12.3 %collective-permute-start.1 = (f32[192,512]{1,0:T(8,128)S(1)}, f32[192,512]{1,0:T(8,128)S(1)}, u32[]{:S(2)}, u32[]{:S(2)}) collective-permute-start(f32[192,512]{1,0:T(8,128)S(1)} %get-tuple-element.61), channel_id=1, source_target_pairs={{0,4},{1,5},{2,6},{3,7},{4,0},{5,1},{6,2},{7,3},{8,12},{9,13},{10,... | collective-permute-start | bytes 1179656 | tf_op jit(solution)/shard_map/ppermute | solution.py:30
  24.4 18.1 %collective-permute-start.3 = (f32[192,512]{1,0:T(8,128)S(1)}, f32[192,512]{1,0:T(8,128)S(1)}, u32[]{:S(2)}, u32[]{:S(2)}) collective-permute-start(f32[192,512]{1,0:T(8,128)S(1)} %get-tuple-element.62), channel_id=1, source_target_pairs={{0,6},{1,7},{2,0},{3,1},{4,2},{5,3},{6,4},{7,5},{8,14},{9,15},{10,... | collective-permute-start | bytes 1179656 | tf_op jit(solution)/shard_map/ppermute | solution.py:30
  25.2 18.0 %collective-permute-start.2 = (f32[192,512]{1,0:T(8,128)S(1)}, f32[192,512]{1,0:T(8,128)}, u32[]{:S(2)}, u32[]{:S(2)}) collective-permute-start(f32[192,512]{1,0:T(8,128)S(1)} %get-tuple-element.63), channel_id=1, source_target_pairs={{0,2},{1,3},{2,4},{3,5},{4,6},{5,7},{6,0},{7,1},{8,10},{9,11},{10,... | collective-permute-start | bytes 1179656 | tf_op jit(solution)/shard_map/ppermute | solution.py:30
  33.7 8.7 %copy-start.7 = (f32[192,512]{1,0:T(8,128)}, f32[192,512]{1,0:T(8,128)S(1)}, u32[]{:S(2)}) copy-start(f32[192,512]{1,0:T(8,128)S(1)} %collective-permute-done.1) | copy-start | bytes 1179652
  42.5 0.7 copy-start.9
  43.2 1.0 copy-start.8
  43.2 1.1 copy-start.10
  45.5 25.7 %copy-start.3 = (f32[16,128]{1,0:T(8,128)S(1)}, f32[16,128]{1,0:T(8,128)}, u32[]{:S(2)}) copy-start(f32[16,128]{1,0:T(8,128)} %get-tuple-element.34.sq_one) | copy-start | bytes 24580
  45.5 25.7 %copy-start.4 = (f32[16,128]{1,0:T(8,128)S(1)}, f32[16,128]{1,0:T(8,128)}, u32[]{:S(2)}) copy-start(f32[16,128]{1,0:T(8,128)} %get-tuple-element.35.sq_two) | copy-start | bytes 24580
  45.5 11.2 %collective-permute-start.4 = (f32[192,512]{1,0:T(8,128)S(1)}, f32[192,512]{1,0:T(8,128)S(1)}, u32[]{:S(2)}, u32[]{:S(2)}) collective-permute-start(f32[192,512]{1,0:T(8,128)S(1)} %get-tuple-element.60), channel_id=1, source_target_pairs={{0,2},{1,3},{2,4},{3,5},{4,6},{5,7},{6,0},{7,1},{8,10},{9,11},{10,... | collective-permute-start | bytes 1179656 | tf_op jit(solution)/shard_map/ppermute | solution.py:30
  47.0 19.5 %collective-permute-start.5 = (f32[192,512]{1,0:T(8,128)S(1)}, f32[192,512]{1,0:T(8,128)S(1)}, u32[]{:S(2)}, u32[]{:S(2)}) collective-permute-start(f32[192,512]{1,0:T(8,128)S(1)} %get-tuple-element.60), channel_id=1, source_target_pairs={{0,4},{1,5},{2,6},{3,7},{4,0},{5,1},{6,2},{7,3},{8,12},{9,13},{10,... | collective-permute-start | bytes 1179656 | tf_op jit(solution)/shard_map/ppermute | solution.py:30
  49.4 17.2 %collective-permute-start.6 = (f32[192,512]{1,0:T(8,128)S(1)}, f32[192,512]{1,0:T(8,128)S(1)}, u32[]{:S(2)}, u32[]{:S(2)}) collective-permute-start(f32[192,512]{1,0:T(8,128)S(1)} %get-tuple-element.60), channel_id=1, source_target_pairs={{0,6},{1,7},{2,0},{3,1},{4,2},{5,3},{6,4},{7,5},{8,14},{9,15},{10,... | collective-permute-start | bytes 1179656 | tf_op jit(solution)/shard_map/ppermute | solution.py:30
  66.6 4.6 %collective-permute-start.7 = (f32[768,512]{1,0:T(8,128)S(1)}, f32[768,512]{1,0:T(8,128)}, u32[]{:S(2)}, u32[]{:S(2)}) collective-permute-start(f32[768,512]{1,0:T(8,128)S(1)} %constant_dynamic-update-slice_fusion.8.own), channel_id=1, source_target_pairs={{0,1},{1,0},{2,3},{3,2},{4,5},{5,4},{6,7},{7,6},{8,9},{9,8},{10,11... | collective-permute-start | bytes 4718600 | tf_op jit(solution)/shard_map/ppermute | solution.py:34
  83.4 0.8 copy-start.5
  84.3 0.8 copy-start.6
  85.0 14.5 %collective-permute-start.8 = (f32[32,3968]{1,0:T(8,128)}, f32[32,3968]{1,0:T(8,128)S(1)}, u32[]{:S(2)}, u32[]{:S(2)}) collective-permute-start(f32[32,3968]{1,0:T(8,128)} %get-tuple-element.37), channel_id=1, source_target_pairs={{0,16},{8,24},{16,0},{24,8},{32,48},{40,56},{48,32},{56,40},{64,80... | collective-permute-start | bytes 1523720 | tf_op jit(solution)/shard_map/ppermute | solution.py:30
  88.0 23.2 %collective-permute-start.9 = (f32[32,3968]{1,0:T(8,128)}, f32[32,3968]{1,0:T(8,128)S(1)}, u32[]{:S(2)}, u32[]{:S(2)}) collective-permute-start(f32[32,3968]{1,0:T(8,128)} %get-tuple-element.38), channel_id=1, source_target_pairs={{0,8},{8,16},{16,24},{24,0},{32,40},{40,48},{48,56},{56,32},{64,72... | collective-permute-start | bytes 1523720 | tf_op jit(solution)/shard_map/ppermute | solution.py:30
  88.4 22.8 %collective-permute-start.10 = (f32[32,3968]{1,0:T(8,128)}, f32[32,3968]{1,0:T(8,128)S(1)}, u32[]{:S(2)}, u32[]{:S(2)}) collective-permute-start(f32[32,3968]{1,0:T(8,128)} %get-tuple-element.39), channel_id=1, source_target_pairs={{0,24},{8,0},{16,8},{24,16},{32,56},{40,32},{48,40},{56,48},{64,88... | collective-permute-start | bytes 1523720 | tf_op jit(solution)/shard_map/ppermute | solution.py:30
  90.6 25.0 %collective-permute-start.14 = (f32[32,3968]{1,0:T(8,128)}, f32[32,3968]{1,0:T(8,128)S(1)}, u32[]{:S(2)}, u32[]{:S(2)}) collective-permute-start(f32[32,3968]{1,0:T(8,128)} %copy-done.6), channel_id=1, source_target_pairs={{0,64},{8,72},{16,80},{24,88},{32,96},{40,104},{48,112},{56,120},{... | collective-permute-start | bytes 1523720 | tf_op jit(solution)/shard_map/ppermute | solution.py:30
  94.3 24.2 %collective-permute-start.15 = (f32[32,3968]{1,0:T(8,128)}, f32[32,3968]{1,0:T(8,128)S(1)}, u32[]{:S(2)}, u32[]{:S(2)}) collective-permute-start(f32[32,3968]{1,0:T(8,128)} %copy-done.5), channel_id=1, source_target_pairs={{0,32},{8,40},{16,48},{24,56},{32,64},{40,72},{48,80},{56,88},{64,... | collective-permute-start | bytes 1523720 | tf_op jit(solution)/shard_map/ppermute | solution.py:30
  99.6 18.9 %collective-permute-start.16 = (f32[32,3968]{1,0:T(8,128)S(1)}, f32[32,3968]{1,0:T(8,128)S(1)}, u32[]{:S(2)}, u32[]{:S(2)}) collective-permute-start(f32[32,3968]{1,0:T(8,128)S(1)} %get-tuple-element.43), channel_id=1, source_target_pairs={{0,96},{8,104},{16,112},{24,120},{32,0},{40,8},{48,16},{56,24},{64... | collective-permute-start | bytes 1523720 | tf_op jit(solution)/shard_map/ppermute | solution.py:30
  111.3 9.3 %collective-permute-start.11 = (f32[8,3968]{1,0:T(8,128)S(1)}, f32[8,3968]{1,0:T(8,128)S(1)}, u32[]{:S(2)}, u32[]{:S(2)}) collective-permute-start(f32[8,3968]{1,0:T(8,128)S(1)} %get-tuple-element.69), channel_id=1, source_target_pairs={{0,64},{8,72},{16,80},{24,88},{32,96},{40,104},{48,112},{56,120},{... | collective-permute-start | bytes 380936 | tf_op jit(solution)/shard_map/ppermute | solution.py:30
  115.0 7.5 %collective-permute-start.13 = (f32[8,3968]{1,0:T(8,128)S(1)}, f32[8,3968]{1,0:T(8,128)S(1)}, u32[]{:S(2)}, u32[]{:S(2)}) collective-permute-start(f32[8,3968]{1,0:T(8,128)S(1)} %get-tuple-element.70), channel_id=1, source_target_pairs={{0,96},{8,104},{16,112},{24,120},{32,0},{40,8},{48,16},{56,24},{64... | collective-permute-start | bytes 380936 | tf_op jit(solution)/shard_map/ppermute | solution.py:30
  115.7 6.8 %collective-permute-start.12 = (f32[8,3968]{1,0:T(8,128)S(1)}, f32[8,3968]{1,0:T(8,128)S(1)}, u32[]{:S(2)}, u32[]{:S(2)}) collective-permute-start(f32[8,3968]{1,0:T(8,128)S(1)} %get-tuple-element.71), channel_id=1, source_target_pairs={{0,32},{8,40},{16,48},{24,56},{32,64},{40,72},{48,80},{56,88},{64,... | collective-permute-start | bytes 380936 | tf_op jit(solution)/shard_map/ppermute | solution.py:30
  118.7 5.4 %collective-permute-start.17 = (f32[8,3968]{1,0:T(8,128)S(1)}, f32[8,3968]{1,0:T(8,128)S(1)}, u32[]{:S(2)}, u32[]{:S(2)}) collective-permute-start(f32[8,3968]{1,0:T(8,128)S(1)} %get-tuple-element.66), channel_id=1, source_target_pairs={{0,16},{8,24},{16,0},{24,8},{32,48},{40,56},{48,32},{56,40},{64,80... | collective-permute-start | bytes 380936 | tf_op jit(solution)/shard_map/ppermute | solution.py:30
  118.8 6.0 %collective-permute-start.19 = (f32[8,3968]{1,0:T(8,128)S(1)}, f32[8,3968]{1,0:T(8,128)S(1)}, u32[]{:S(2)}, u32[]{:S(2)}) collective-permute-start(f32[8,3968]{1,0:T(8,128)S(1)} %get-tuple-element.67), channel_id=1, source_target_pairs={{0,24},{8,0},{16,8},{24,16},{32,56},{40,32},{48,40},{56,48},{64,88... | collective-permute-start | bytes 380936 | tf_op jit(solution)/shard_map/ppermute | solution.py:30
  120.6 6.6 %collective-permute-start.18 = (f32[8,3968]{1,0:T(8,128)S(1)}, f32[8,3968]{1,0:T(8,128)S(1)}, u32[]{:S(2)}, u32[]{:S(2)}) collective-permute-start(f32[8,3968]{1,0:T(8,128)S(1)} %get-tuple-element.68), channel_id=1, source_target_pairs={{0,8},{8,16},{16,24},{24,0},{32,40},{40,48},{48,56},{56,32},{64,72... | collective-permute-start | bytes 380936 | tf_op jit(solution)/shard_map/ppermute | solution.py:30
  128.0 143.6 %all-gather.3.cloned.1.call-start = ((), (), s32[]{:S(2)}) async-start(), calls=%async_computation.1 | async-start | bytes 3342336 | tf_op jit(solution)/shard_map/all_gather | solution.py:575
  128.0 6.2 %collective-permute-start.20 = (f32[48,256]{1,0:T(8,128)S(1)}, f32[48,256]{1,0:T(8,128)S(1)}, u32[]{:S(2)}, u32[]{:S(2)}) collective-permute-start(f32[48,256]{1,0:T(8,128)S(1)} %pad_maximum_fusion.4), channel_id=1, source_target_pairs={{0,0},{1,16},{2,32},{3,48},{4,64},{5,80},{6,96},{7,112},{8,2},{9,1... | collective-permute-start | bytes 147464 | tf_op jit(solution)/shard_map/ppermute | solution.py:116
  134.2 10.5 %collective-permute-start.23 = (f32[48,256]{1,0:T(8,128)S(1)}, f32[48,256]{1,0:T(8,128)S(1)}, u32[]{:S(2)}, u32[]{:S(2)}) collective-permute-start(f32[48,256]{1,0:T(8,128)S(1)} %collective-permute-done.20), channel_id=1, source_target_pairs={{0,6},{1,7},{2,0},{3,1},{4,2},{5,3},{6,4},{7,5},{8,14},{9,15},{10,... | collective-permute-start | bytes 147464 | tf_op jit(solution)/shard_map/ppermute | solution.py:30
  140.0 4.7 %collective-permute-start.22 = (f32[48,256]{1,0:T(8,128)S(1)}, f32[48,256]{1,0:T(8,128)S(1)}, u32[]{:S(2)}, u32[]{:S(2)}) collective-permute-start(f32[48,256]{1,0:T(8,128)S(1)} %collective-permute-done.20), channel_id=1, source_target_pairs={{0,4},{1,5},{2,6},{3,7},{4,0},{5,1},{6,2},{7,3},{8,12},{9,13},{10,... | collective-permute-start | bytes 147464 | tf_op jit(solution)/shard_map/ppermute | solution.py:30
  140.0 4.7 %collective-permute-start.21 = (f32[48,256]{1,0:T(8,128)S(1)}, f32[48,256]{1,0:T(8,128)S(1)}, u32[]{:S(2)}, u32[]{:S(2)}) collective-permute-start(f32[48,256]{1,0:T(8,128)S(1)} %collective-permute-done.20), channel_id=1, source_target_pairs={{0,2},{1,3},{2,4},{3,5},{4,6},{5,7},{6,0},{7,1},{8,10},{9,11},{10,... | collective-permute-start | bytes 147464 | tf_op jit(solution)/shard_map/ppermute | solution.py:30
  144.7 3.9 %collective-permute-start.24 = (f32[192,256]{1,0:T(8,128)S(1)}, f32[192,256]{1,0:T(8,128)S(1)}, u32[]{:S(2)}, u32[]{:S(2)}) collective-permute-start(f32[192,256]{1,0:T(8,128)S(1)} %constant_dynamic-update-slice_fusion.4), channel_id=1, source_target_pairs={{0,1},{1,0},{2,3},{3,2},{4,5},{5,4},{6,7},{7,6},{8,9},{9,8},{10,11... | collective-permute-start | bytes 589832 | tf_op jit(solution)/shard_map/ppermute | solution.py:34
  154.3 15.0 %collective-permute-start.25 = (f32[32,3072]{1,0:T(8,128)S(1)}, f32[32,3072]{1,0:T(8,128)S(1)}, u32[]{:S(2)}, u32[]{:S(2)}) collective-permute-start(f32[32,3072]{1,0:T(8,128)S(1)} %get-tuple-element.45), channel_id=1, source_target_pairs={{0,16},{8,24},{16,0},{24,8},{32,48},{40,56},{48,32},{56,40},{64,80... | collective-permute-start | bytes 1179656 | tf_op jit(solution)/shard_map/ppermute | solution.py:30
  154.7 29.0 %collective-permute-start.26 = (f32[32,3072]{1,0:T(8,128)S(1)}, f32[32,3072]{1,0:T(8,128)S(1)}, u32[]{:S(2)}, u32[]{:S(2)}) collective-permute-start(f32[32,3072]{1,0:T(8,128)S(1)} %get-tuple-element.46), channel_id=1, source_target_pairs={{0,8},{8,16},{16,24},{24,0},{32,40},{40,48},{48,56},{56,32},{64,72... | collective-permute-start | bytes 1179656 | tf_op jit(solution)/shard_map/ppermute | solution.py:30
  156.9 27.0 %collective-permute-start.27 = (f32[32,3072]{1,0:T(8,128)S(1)}, f32[32,3072]{1,0:T(8,128)S(1)}, u32[]{:S(2)}, u32[]{:S(2)}) collective-permute-start(f32[32,3072]{1,0:T(8,128)S(1)} %get-tuple-element.47), channel_id=1, source_target_pairs={{0,24},{8,0},{16,8},{24,16},{32,56},{40,32},{48,40},{56,48},{64,88... | collective-permute-start | bytes 1179656 | tf_op jit(solution)/shard_map/ppermute | solution.py:30
  158.8 33.5 %collective-permute-start.31 = (f32[32,3072]{1,0:T(8,128)S(1)}, f32[32,3072]{1,0:T(8,128)S(1)}, u32[]{:S(2)}, u32[]{:S(2)}) collective-permute-start(f32[32,3072]{1,0:T(8,128)S(1)} %get-tuple-element.49), channel_id=1, source_target_pairs={{0,64},{8,72},{16,80},{24,88},{32,96},{40,104},{48,112},{56,120},{... | collective-permute-start | bytes 1179656 | tf_op jit(solution)/shard_map/ppermute | solution.py:30
  160.3 32.5 %collective-permute-start.32 = (f32[32,3072]{1,0:T(8,128)S(1)}, f32[32,3072]{1,0:T(8,128)S(1)}, u32[]{:S(2)}, u32[]{:S(2)}) collective-permute-start(f32[32,3072]{1,0:T(8,128)S(1)} %get-tuple-element.50), channel_id=1, source_target_pairs={{0,32},{8,40},{16,48},{24,56},{32,64},{40,72},{48,80},{56,88},{64,... | collective-permute-start | bytes 1179656 | tf_op jit(solution)/shard_map/ppermute | solution.py:30
  169.3 25.1 %collective-permute-start.33 = (f32[32,3072]{1,0:T(8,128)S(1)}, f32[32,3072]{1,0:T(8,128)S(1)}, u32[]{:S(2)}, u32[]{:S(2)}) collective-permute-start(f32[32,3072]{1,0:T(8,128)S(1)} %get-tuple-element.51), channel_id=1, source_target_pairs={{0,96},{8,104},{16,112},{24,120},{32,0},{40,8},{48,16},{56,24},{64... | collective-permute-start | bytes 1179656 | tf_op jit(solution)/shard_map/ppermute | solution.py:30
  184.0 14.0 %collective-permute-start.28 = (f32[8,3072]{1,0:T(8,128)S(1)}, f32[8,3072]{1,0:T(8,128)S(1)}, u32[]{:S(2)}, u32[]{:S(2)}) collective-permute-start(f32[8,3072]{1,0:T(8,128)S(1)} %get-tuple-element.75), channel_id=1, source_target_pairs={{0,64},{8,72},{16,80},{24,88},{32,96},{40,104},{48,112},{56,120},{... | collective-permute-start | bytes 294920 | tf_op jit(solution)/shard_map/ppermute | solution.py:30
  186.2 12.4 %collective-permute-start.30 = (f32[8,3072]{1,0:T(8,128)S(1)}, f32[8,3072]{1,0:T(8,128)S(1)}, u32[]{:S(2)}, u32[]{:S(2)}) collective-permute-start(f32[8,3072]{1,0:T(8,128)S(1)} %get-tuple-element.76), channel_id=1, source_target_pairs={{0,96},{8,104},{16,112},{24,120},{32,0},{40,8},{48,16},{56,24},{64... | collective-permute-start | bytes 294920 | tf_op jit(solution)/shard_map/ppermute | solution.py:30
  192.3 6.7 %collective-permute-start.29 = (f32[8,3072]{1,0:T(8,128)S(1)}, f32[8,3072]{1,0:T(8,128)S(1)}, u32[]{:S(2)}, u32[]{:S(2)}) collective-permute-start(f32[8,3072]{1,0:T(8,128)S(1)} %get-tuple-element.77), channel_id=1, source_target_pairs={{0,32},{8,40},{16,48},{24,56},{32,64},{40,72},{48,80},{56,88},{64,... | collective-permute-start | bytes 294920 | tf_op jit(solution)/shard_map/ppermute | solution.py:30
  194.5 5.1 %collective-permute-start.34 = (f32[8,3072]{1,0:T(8,128)S(1)}, f32[8,3072]{1,0:T(8,128)S(1)}, u32[]{:S(2)}, u32[]{:S(2)}) collective-permute-start(f32[8,3072]{1,0:T(8,128)S(1)} %get-tuple-element.78), channel_id=1, source_target_pairs={{0,16},{8,24},{16,0},{24,8},{32,48},{40,56},{48,32},{56,40},{64,80... | collective-permute-start | bytes 294920 | tf_op jit(solution)/shard_map/ppermute | solution.py:30
  197.2 3.7 %collective-permute-start.36 = (f32[8,3072]{1,0:T(8,128)S(1)}, f32[8,3072]{1,0:T(8,128)S(1)}, u32[]{:S(2)}, u32[]{:S(2)}) collective-permute-start(f32[8,3072]{1,0:T(8,128)S(1)} %get-tuple-element.79), channel_id=1, source_target_pairs={{0,24},{8,0},{16,8},{24,16},{32,56},{40,32},{48,40},{56,48},{64,88... | collective-permute-start | bytes 294920 | tf_op jit(solution)/shard_map/ppermute | solution.py:30
  198.0 5.5 %collective-permute-start.35 = (f32[8,3072]{1,0:T(8,128)S(1)}, f32[8,3072]{1,0:T(8,128)S(1)}, u32[]{:S(2)}, u32[]{:S(2)}) collective-permute-start(f32[8,3072]{1,0:T(8,128)S(1)} %get-tuple-element.80), channel_id=1, source_target_pairs={{0,8},{8,16},{16,24},{24,0},{32,40},{40,48},{48,56},{56,32},{64,72... | collective-permute-start | bytes 294920 | tf_op jit(solution)/shard_map/ppermute | solution.py:30
  213.1 15.6 %copy-start.1 = (f32[64,256]{1,0:T(8,128)S(1)}, f32[64,256]{1,0:T(8,128)}, u32[]{:S(2)}) copy-start(f32[64,256]{1,0:T(8,128)} %get-tuple-element.53.cores) | copy-start | bytes 196612
  213.1 15.6 %copy-start.2 = (f32[16,256]{1,0:T(8,128)S(1)}, f32[16,256]{1,0:T(8,128)}, u32[]{:S(2)}) copy-start(f32[16,256]{1,0:T(8,128)} %get-tuple-element.54.both) | copy-start | bytes 49156
  213.1 5.4 %collective-permute-start.37 = (f32[480,256]{1,0:T(8,128)S(1)}, f32[480,256]{1,0:T(8,128)S(1)}, u32[]{:S(2)}, u32[]{:S(2)}) collective-permute-start(f32[480,256]{1,0:T(8,128)S(1)} %constant_dynamic-slice_fusion.3), channel_id=1, source_target_pairs={{0,1},{1,0},{2,3},{3,2},{4,5},{5,4},{6,7},{7,6},{8,9},{9,8},{10,11... | collective-permute-start | bytes 1474568 | tf_op jit(solution)/shard_map/ppermute | solution.py:34
  219.7 6.1 %collective-permute-start.38 = (f32[120,256]{1,0:T(8,128)S(1)}, f32[120,256]{1,0:T(8,128)S(1)}, u32[]{:S(2)}, u32[]{:S(2)}) collective-permute-start(f32[120,256]{1,0:T(8,128)S(1)} %get-tuple-element.72), channel_id=1, source_target_pairs={{0,4},{1,5},{2,6},{3,7},{4,0},{5,1},{6,2},{7,3},{8,12},{9,13},{10,... | collective-permute-start | bytes 368648 | tf_op jit(solution)/shard_map/ppermute | solution.py:30
  220.4 5.8 %collective-permute-start.40 = (f32[120,256]{1,0:T(8,128)S(1)}, f32[120,256]{1,0:T(8,128)S(1)}, u32[]{:S(2)}, u32[]{:S(2)}) collective-permute-start(f32[120,256]{1,0:T(8,128)S(1)} %get-tuple-element.73), channel_id=1, source_target_pairs={{0,6},{1,7},{2,0},{3,1},{4,2},{5,3},{6,4},{7,5},{8,14},{9,15},{10,... | collective-permute-start | bytes 368648 | tf_op jit(solution)/shard_map/ppermute | solution.py:30
  221.4 7.3 %collective-permute-start.39 = (f32[120,256]{1,0:T(8,128)S(1)}, f32[120,256]{1,0:T(8,128)S(1)}, u32[]{:S(2)}, u32[]{:S(2)}) collective-permute-start(f32[120,256]{1,0:T(8,128)S(1)} %get-tuple-element.74), channel_id=1, source_target_pairs={{0,2},{1,3},{2,4},{3,5},{4,6},{5,7},{6,0},{7,1},{8,10},{9,11},{10,... | collective-permute-start | bytes 368648 | tf_op jit(solution)/shard_map/ppermute | solution.py:30
  228.9 15.6 %collective-permute-start.41 = (f32[128,256]{1,0:T(8,128)S(1)}, f32[128,256]{1,0:T(8,128)S(1)}, u32[]{:S(2)}, u32[]{:S(2)}) collective-permute-start(f32[128,256]{1,0:T(8,128)S(1)} %get-tuple-element.55), channel_id=1, source_target_pairs={{0,2},{1,3},{2,4},{3,5},{4,6},{5,7},{6,0},{7,1},{8,10},{9,11},{10,... | collective-permute-start | bytes 393224 | tf_op jit(solution)/shard_map/ppermute | solution.py:30
  239.2 8.0 %collective-permute-start.43 = (f32[128,256]{1,0:T(8,128)S(1)}, f32[128,256]{1,0:T(8,128)S(1)}, u32[]{:S(2)}, u32[]{:S(2)}) collective-permute-start(f32[128,256]{1,0:T(8,128)S(1)} %get-tuple-element.55), channel_id=1, source_target_pairs={{0,6},{1,7},{2,0},{3,1},{4,2},{5,3},{6,4},{7,5},{8,14},{9,15},{10,... | collective-permute-start | bytes 393224 | tf_op jit(solution)/shard_map/ppermute | solution.py:30
  241.8 5.4 %collective-permute-start.42 = (f32[128,256]{1,0:T(8,128)S(1)}, f32[128,256]{1,0:T(8,128)S(1)}, u32[]{:S(2)}, u32[]{:S(2)}) collective-permute-start(f32[128,256]{1,0:T(8,128)S(1)} %get-tuple-element.55), channel_id=1, source_target_pairs={{0,4},{1,5},{2,6},{3,7},{4,0},{5,1},{6,2},{7,3},{8,12},{9,13},{10,... | collective-permute-start | bytes 393224 | tf_op jit(solution)/shard_map/ppermute | solution.py:30
  247.2 4.2 %collective-permute-start.44 = (f32[512,256]{1,0:T(8,128)S(1)}, f32[512,256]{1,0:T(8,128)S(1)}, u32[]{:S(2)}, u32[]{:S(2)}) collective-permute-start(f32[512,256]{1,0:T(8,128)S(1)} %constant_dynamic-update-slice_fusion), channel_id=1, source_target_pairs={{0,1},{1,0},{2,3},{3,2},{4,5},{5,4},{6,7},{7,6},{8,9},{9,8},{10,11... | collective-permute-start | bytes 1572872 | tf_op jit(solution)/shard_map/ppermute | solution.py:34
  252.3 19.3 %all-to-all-start = ((f32[16,16,256]{2,1,0:T(8,128)}), f32[16,16,256]{2,1,0:T(8,128)S(1)}, u32[]{:S(2)}, u32[]{:S(2)}) async-start(f32[16,16,256]{2,1,0:T(8,128)} %bitcast.5), calls=%async_computation | async-start | bytes 524288 | tf_op jit(solution)/shard_map/all_to_all | solution.py:581
  271.6 1.9 copy-start
Sparse Core Ops, SparseCore 0:
  128.1 68.9 all-gather.4
  204.4 48.3 all-gather.2

commit v2 on v1

--- a/solution.py
+++ b/solution.py
@@ -14,6 +14,7 @@
 BLOCK = 64
 VMEM_LIMIT = 48 * 1024 * 1024
 VMEM_MOST = 60 * 1024 * 1024
+VMEM_LAST = 58 * 1024 * 1024
 
 DAMPING = 0.1
 
@@ -542,6 +543,7 @@
         out_specs=pl.BlockSpec((count, TILE), lambda j: (0, j)),
         scratch_shapes=[pltpu.VMEM((count, R), jnp.float32)]
         + [pltpu.VMEM((count, R), jnp.bfloat16)] * 4,
+        vmem=VMEM_LAST,
         name="last_update",
     )(left_sums, weight, range_grad, *rest)
 

time: 294 us -> 297 us (1.010)
    unnamed x22 -> x32, local copies, waits for them, and re-layouts: 5.19 us -> 5.96 us
where the time goes in v2:
time: 297 us; the launch traced here: 293 us
  starting transfers between devices  102 us (34%)
  waiting for transfers between devices  99.3 us (33%)
  Pallas kernels  63.6 us (21%)
  between operations  14.1 us (5%)
  local copies, waits for them, and re-layouts  7.75 us (3%)
  other arithmetic  6.17 us (2%)
    ppermute x39, waiting for transfers between devices, send(): lax.ppermute(value, 'tensor' if kind == 'x' else 'dp', ring(kind, step))  89.8 us
    ppermute x39, starting transfers between devices, send(): lax.ppermute(value, 'tensor' if kind == 'x' else 'dp', ring(kind, step))  80.3 us
    pallas_call x1, Pallas kernels, factors(): call(factor_kernel, [array(R, R), array(R, R)], in_specs=[whole], out_spe...  14 us
    ppermute x5, starting transfers between devices, swap_cores(): return lax.ppermute(value, 'tensor', [(i, i ^ 1) for i in range(8)])  12.2 us
    pallas_call x1, Pallas kernels, ranges(): call(functools.partial(ranges_kernel, tokens_all), [array(R // 8, total)]...  12.2 us
    pallas_call x2, Pallas kernels, sketches(): call(sketch_kernel, [array(count, 2 * R), array(16, 128)], vmem=VMEM_MOST...  11.6 us
    pallas_call x1, Pallas kernels, last_update(): call(last_kernel, array(count, columns), grid=(columns // TILE,), in_spec...  11.5 us
    pallas_call x1, Pallas kernels, right_products(): call(right_kernel, [array(960, R), array(64, R), array(16, R)], grid=(col...  7.71 us
  transfers between devices with their start and end apart: 48, of which 30 were waited for; matrix products, arithmetic and copies ran while one was open for 1% of the time, Pallas kernels for 12%

profile of v2, /device:TPU:1, one launch (start us, length us, event | category | flops | bytes accessed | tf_op | source)
XLA Modules:
  0.0 292.6 jit_solution(555114106544133510)
XLA Ops:
  6.5 5.8 %sketches.3 = (f32[768,512]{1,0:T(8,128)}, f32[16,128]{1,0:T(8,128)}) custom-call(s32[1]{0:T(128)} %bitcast.4.core, bf16[1536,3072]{1,0:T(8,128)(2,1)} %grads.5, bf16[1536,768]{1,0:T(8,128)(2,1)} %acts.5, bf16[3072,256]{1,0:T(8,128)(2,1)} %sketch_out.3, bf16[768,256]{1,0:T(8,128)(2,1)} %sketch_in.3), custom_call_target="tpu_custom_call" | custom-call | tf_op jit(solution)/shard_map/sketches/pallas_call | solution.py:210
  12.3 1.4 collective-permute-start
  13.8 5.8 %sketches.2 = (f32[768,512]{1,0:T(8,128)}, f32[16,128]{1,0:T(8,128)}) custom-call(s32[1]{0:T(128)} %bitcast.1.core, bf16[1536,3072]{1,0:T(8,128)(2,1)} %grads.5, bf16[1536,768]{1,0:T(8,128)(2,1)} %acts.5, bf16[3072,256]{1,0:T(8,128)(2,1)} %sketch_out.3, bf16[768,256]{1,0:T(8,128)(2,1)} %sketch_in.3), custom_call_target="tpu_custom_call" | custom-call | tf_op jit(solution)/shard_map/sketches/pallas_call | solution.py:210
  19.6 1.8 add.318
  21.4 2.9 collective-permute-start.1
  25.8 7.9 %collective-permute-done.1 = f32[192,512]{1,0:T(8,128)S(1)} collective-permute-done((f32[192,512]{1,0:T(8,128)S(1)}, f32[192,512]{1,0:T(8,128)S(1)}, u32[]{:S(2)}, u32[]{:S(2)}) %collective-permute-start.1) | collective-permute-done | bytes 393248 | tf_op jit(solution)/shard_map/ppermute | solution.py:31
  33.7 8.6 %collective-permute-done.3 = f32[192,512]{1,0:T(8,128)S(1)} collective-permute-done((f32[192,512]{1,0:T(8,128)S(1)}, f32[192,512]{1,0:T(8,128)S(1)}, u32[]{:S(2)}, u32[]{:S(2)}) %collective-permute-start.3) | collective-permute-done | bytes 393248 | tf_op jit(solution)/shard_map/ppermute | solution.py:31
  44.2 1.1 constant_dynamic-update-slice_fusion.11
  45.3 1.6 collective-permute-start.4
  47.0 2.3 collective-permute-start.5
  49.8 6.7 %collective-permute-done.4 = f32[192,512]{1,0:T(8,128)S(1)} collective-permute-done((f32[192,512]{1,0:T(8,128)S(1)}, f32[192,512]{1,0:T(8,128)S(1)}, u32[]{:S(2)}, u32[]{:S(2)}) %collective-permute-start.4) | collective-permute-done | bytes 393248 | tf_op jit(solution)/shard_map/ppermute | solution.py:31
  56.6 9.9 %collective-permute-done.5 = f32[192,512]{1,0:T(8,128)S(1)} collective-permute-done((f32[192,512]{1,0:T(8,128)S(1)}, f32[192,512]{1,0:T(8,128)S(1)}, u32[]{:S(2)}, u32[]{:S(2)}) %collective-permute-start.5) | collective-permute-done | bytes 393248 | tf_op jit(solution)/shard_map/ppermute | solution.py:31
  66.6 1.4 collective-permute-start.7
  68.1 3.1 %collective-permute-done.7.other = f32[768,512]{1,0:T(8,128)} collective-permute-done((f32[768,512]{1,0:T(8,128)S(1)}, f32[768,512]{1,0:T(8,128)}, u32[]{:S(2)}, u32[]{:S(2)}) %collective-permute-start.7) | collective-permute-done | bytes 1572896 | tf_op jit(solution)/shard_map/ppermute | solution.py:35
  71.2 12.2 %ranges.1 = (f32[32,3968]{1,0:T(8,128)S(1)}, f32[32,3968]{1,0:T(8,128)}, f32[32,3968]{1,0:T(8,128)}, f32[32,3968]{1,0:T(8,128)}, f32[32,3968]{1,0:T(8,128)S(1)},...) custom-call(s32[4]{0:T(128)S(1)} %pad_add_fusion.places, ...), custom_call_target="tpu_custom_call" | custom-call | tf_op jit(solution)/shard_map/ranges/pallas_call | solution.py:292
  85.0 2.9 %collective-permute-start.8 = (f32[32,3968]{1,0:T(8,128)}, f32[32,3968]{1,0:T(8,128)S(1)}, u32[]{:S(2)}, u32[]{:S(2)}) collective-permute-start(f32[32,3968]{1,0:T(8,128)} %get-tuple-element.37), channel_id=1, source_target_pairs={{0,16},{8,24},{16,0},{24,8},{32,48},{40,56},{48,32},{56,40},{64,80... | collective-permute-start | bytes 1523720 | tf_op jit(solution)/shard_map/ppermute | solution.py:31
  88.3 2.3 collective-permute-start.10
  90.6 3.6 %collective-permute-start.14 = (f32[32,3968]{1,0:T(8,128)}, f32[32,3968]{1,0:T(8,128)S(1)}, u32[]{:S(2)}, u32[]{:S(2)}) collective-permute-start(f32[32,3968]{1,0:T(8,128)} %copy-done.10), channel_id=1, source_target_pairs={{0,64},{8,72},{16,80},{24,88},{32,96},{40,104},{48,112},{56,120},{... | collective-permute-start | bytes 1523720 | tf_op jit(solution)/shard_map/ppermute | solution.py:31
  95.0 4.6 %collective-permute-done.8 = f32[32,3968]{1,0:T(8,128)S(1)} collective-permute-done((f32[32,3968]{1,0:T(8,128)}, f32[32,3968]{1,0:T(8,128)S(1)}, u32[]{:S(2)}, u32[]{:S(2)}) %collective-permute-start.8) | collective-permute-done | bytes 507936 | tf_op jit(solution)/shard_map/ppermute | solution.py:31
  99.5 3.8 %collective-permute-start.16 = (f32[32,3968]{1,0:T(8,128)S(1)}, f32[32,3968]{1,0:T(8,128)S(1)}, u32[]{:S(2)}, u32[]{:S(2)}) collective-permute-start(f32[32,3968]{1,0:T(8,128)S(1)} %get-tuple-element.43), channel_id=1, source_target_pairs={{0,96},{8,104},{16,112},{24,120},{32,0},{40,8},{48,16},{56,24},{64... | collective-permute-start | bytes 1523720 | tf_op jit(solution)/shard_map/ppermute | solution.py:31
  103.4 7.7 %collective-permute-done.9 = f32[32,3968]{1,0:T(8,128)S(1)} collective-permute-done((f32[32,3968]{1,0:T(8,128)}, f32[32,3968]{1,0:T(8,128)S(1)}, u32[]{:S(2)}, u32[]{:S(2)}) %collective-permute-start.9) | collective-permute-done | bytes 507936 | tf_op jit(solution)/shard_map/ppermute | solution.py:31
  111.2 3.7 %collective-permute-start.11 = (f32[8,3968]{1,0:T(8,128)S(1)}, f32[8,3968]{1,0:T(8,128)S(1)}, u32[]{:S(2)}, u32[]{:S(2)}) collective-permute-start(f32[8,3968]{1,0:T(8,128)S(1)} %get-tuple-element.69), channel_id=1, source_target_pairs={{0,64},{8,72},{16,80},{24,88},{32,96},{40,104},{48,112},{56,120},{... | collective-permute-start | bytes 380936 | tf_op jit(solution)/shard_map/ppermute | solution.py:31
  115.6 1.0 collective-permute-start.12
  116.7 1.8 collective-permute-done.15
  118.7 1.9 collective-permute-start.19
  120.6 1.9 collective-permute-done.13
  122.5 1.4 collective-permute-done.17
  124.7 2.4 collective-permute-done.18
  128.0 3.9 %collective-permute-start.20 = (f32[48,256]{1,0:T(8,128)S(1)}, f32[48,256]{1,0:T(8,128)S(1)}, u32[]{:S(2)}, u32[]{:S(2)}) collective-permute-start(f32[48,256]{1,0:T(8,128)S(1)} %pad_maximum_fusion.4), channel_id=1, source_target_pairs={{0,0},{1,16},{2,32},{3,48},{4,64},{5,80},{6,96},{7,112},{8,2},{9,1... | collective-permute-start | bytes 147464 | tf_op jit(solution)/shard_map/ppermute | solution.py:117
  132.0 2.2 collective-permute-done.20
  134.1 5.9 %collective-permute-start.23 = (f32[48,256]{1,0:T(8,128)S(1)}, f32[48,256]{1,0:T(8,128)S(1)}, u32[]{:S(2)}, u32[]{:S(2)}) collective-permute-start(f32[48,256]{1,0:T(8,128)S(1)} %collective-permute-done.20), channel_id=1, source_target_pairs={{0,6},{1,7},{2,0},{3,1},{4,2},{5,3},{6,4},{7,5},{8,14},{9,15},{10,... | collective-permute-start | bytes 147464 | tf_op jit(solution)/shard_map/ppermute | solution.py:31
  140.9 3.8 %collective-permute-done.21 = f32[48,256]{1,0:T(8,128)S(1)} collective-permute-done((f32[48,256]{1,0:T(8,128)S(1)}, f32[48,256]{1,0:T(8,128)S(1)}, u32[]{:S(2)}, u32[]{:S(2)}) %collective-permute-start.21) | collective-permute-done | bytes 49184 | tf_op jit(solution)/shard_map/ppermute | solution.py:31
  144.7 2.8 collective-permute-start.24
  147.5 1.1 collective-permute-done.24
  148.7 5.6 %left_products.1 = (f32[32,3072]{1,0:T(8,128)S(1)}, f32[32,3072]{1,0:T(8,128)S(1)}, f32[32,3072]{1,0:T(8,128)S(1)}, f32[32,3072]{1,0:T(8,128)S(1)}, f32[32,3072]...) custom-call(s32[4]{0:T(128)S(1)} %pad_add_fusion.places, ...), custom_call_target="tpu_custom_call" | custom-call | tf_op jit(solution)/shard_map/left_products/pallas_call | solution.py:326
  154.7 2.2 collective-permute-start.26
  156.9 1.9 collective-permute-start.27
  158.8 1.6 collective-permute-start.31
  160.4 2.3 collective-permute-start.32
  162.7 6.5 %collective-permute-done.25 = f32[32,3072]{1,0:T(8,128)S(1)} collective-permute-done((f32[32,3072]{1,0:T(8,128)S(1)}, f32[32,3072]{1,0:T(8,128)S(1)}, u32[]{:S(2)}, u32[]{:S(2)}) %collective-permute-start.25) | collective-permute-done | bytes 393248 | tf_op jit(solution)/shard_map/ppermute | solution.py:31
  169.2 7.4 %collective-permute-start.33 = (f32[32,3072]{1,0:T(8,128)S(1)}, f32[32,3072]{1,0:T(8,128)S(1)}, u32[]{:S(2)}, u32[]{:S(2)}) collective-permute-start(f32[32,3072]{1,0:T(8,128)S(1)} %get-tuple-element.51), channel_id=1, source_target_pairs={{0,96},{8,104},{16,112},{24,120},{32,0},{40,8},{48,16},{56,24},{64... | collective-permute-start | bytes 1179656 | tf_op jit(solution)/shard_map/ppermute | solution.py:31
  176.6 7.1 %collective-permute-done.26 = f32[32,3072]{1,0:T(8,128)S(1)} collective-permute-done((f32[32,3072]{1,0:T(8,128)S(1)}, f32[32,3072]{1,0:T(8,128)S(1)}, u32[]{:S(2)}, u32[]{:S(2)}) %collective-permute-start.26) | collective-permute-done | bytes 393248 | tf_op jit(solution)/shard_map/ppermute | solution.py:31
  184.0 2.2 collective-permute-start.28
  186.2 6.1 %collective-permute-start.30 = (f32[8,3072]{1,0:T(8,128)S(1)}, f32[8,3072]{1,0:T(8,128)S(1)}, u32[]{:S(2)}, u32[]{:S(2)}) collective-permute-start(f32[8,3072]{1,0:T(8,128)S(1)} %get-tuple-element.76), channel_id=1, source_target_pairs={{0,96},{8,104},{16,112},{24,120},{32,0},{40,8},{48,16},{56,24},{64... | collective-permute-start | bytes 294920 | tf_op jit(solution)/shard_map/ppermute | solution.py:31
  192.8 1.6 collective-permute-done.33
  194.5 2.7 collective-permute-start.34
  199.6 1.1 collective-permute-done.36
  200.7 2.8 collective-permute-done.35
  204.3 7.7 %right_products.1 = (f32[960,256]{1,0:T(8,128)}, f32[64,256]{1,0:T(8,128)}, f32[16,256]{1,0:T(8,128)}) custom-call(f32[256,3968]{1,0:T(8,128)} %all-gather.5.cloned.1.call-done.whole.refs_0_.refs_1_.refs_2_.refs_3_.refs_4_.refs_5_.refs_6_.range_grad, ...), custom_call_target="tpu_custom_call" | custom-call | tf_op jit(solution)/shard_map/right_products/pallas_call | solution.py:362
  212.0 1.1 constant_dynamic-slice_fusion.3
  213.1 3.9 %collective-permute-start.37 = (f32[480,256]{1,0:T(8,128)S(1)}, f32[480,256]{1,0:T(8,128)S(1)}, u32[]{:S(2)}, u32[]{:S(2)}) collective-permute-start(f32[480,256]{1,0:T(8,128)S(1)} %constant_dynamic-slice_fusion.3), channel_id=1, source_target_pairs={{0,1},{1,0},{2,3},{3,2},{4,5},{5,4},{6,7},{7,6},{8,9},{9,8},{10,11... | collective-permute-start | bytes 1474568 | tf_op jit(solution)/shard_map/ppermute | solution.py:35
  217.0 1.5 collective-permute-done.37
  218.5 1.1 dynamic-slice_add_fusion
  221.9 3.9 %collective-permute-done.38 = f32[120,256]{1,0:T(8,128)S(1)} collective-permute-done((f32[120,256]{1,0:T(8,128)S(1)}, f32[120,256]{1,0:T(8,128)S(1)}, u32[]{:S(2)}, u32[]{:S(2)}) %collective-permute-start.38) | collective-permute-done | bytes 122912 | tf_op jit(solution)/shard_map/ppermute | solution.py:31
  226.3 2.5 collective-permute-done.39
  229.5 9.9 %collective-permute-start.41 = (f32[128,256]{1,0:T(8,128)S(1)}, f32[128,256]{1,0:T(8,128)S(1)}, u32[]{:S(2)}, u32[]{:S(2)}) collective-permute-start(f32[128,256]{1,0:T(8,128)S(1)} %get-tuple-element.55), channel_id=1, source_target_pairs={{0,2},{1,3},{2,4},{3,5},{4,6},{5,7},{6,0},{7,1},{8,10},{9,11},{10,... | collective-permute-start | bytes 393224 | tf_op jit(solution)/shard_map/ppermute | solution.py:31
  239.5 2.6 collective-permute-start.43
  242.2 2.6 collective-permute-done.41
  244.8 2.7 collective-permute-done.42
  247.5 2.7 collective-permute-start.44
  250.2 1.5 collective-permute-done.44
  252.7 5.2 %all-to-all-start = ((f32[16,16,256]{2,1,0:T(8,128)}), f32[16,16,256]{2,1,0:T(8,128)S(1)}, u32[]{:S(2)}, u32[]{:S(2)}) async-start(f32[16,16,256]{2,1,0:T(8,128)} %bitcast.5), calls=%async_computation | async-start | bytes 524288 | tf_op jit(solution)/shard_map/all_to_all | solution.py:583
  257.9 14.0 %factors.1 = (f32[256,256]{1,0:T(8,128)S(1)}, f32[256,256]{1,0:T(8,128)S(1)}) custom-call(f32[1024,256]{1,0:T(8,128)S(1)} %pad_maximum_fusion.right), custom_call_target="tpu_custom_call" | custom-call | tf_op jit(solution)/shard_map/factors/pallas_call | solution.py:497
  274.0 11.5 %last_update.1 = f32[384,3072]{1,0:T(8,128)} custom-call(f32[256,3072]{1,0:T(8,128)} %all-gather.3.cloned.1.call-done.left_sums, f32[384,3072]{1,0:T(8,128)} %weight.3, f32[256,3968]{1,0:T(8,128)} %all-gather.5.cloned.1.call-done.whole.refs_0_.refs_1_.refs_2_.refs_3_.refs_4_.refs_5_.refs_6_.range_grad, f32[1024,256]{1,0:T(8,128)} %copy-done, ...), custom_call_target="tpu_custom_call" | custom-call | tf_op jit(solution)/shard_map/last_update/pallas_call | solution.py:533
  (117 shorter events, 21.7 us)
Async XLA Ops:
  6.5 197.8 %all-gather.5.cloned.1.call-start = ((), (), s32[]{:S(2)}) async-start(), calls=%async_computation.2 | async-start | bytes 4317184 | tf_op jit(solution)/shard_map/all_gather | solution.py:570
  12.3 7.2 %collective-permute-start = (f32[768,512]{1,0:T(8,128)}, f32[768,512]{1,0:T(8,128)S(1)}, u32[]{:S(2)}, u32[]{:S(2)}) collective-permute-start(f32[768,512]{1,0:T(8,128)} %get-tuple-element.33), channel_id=1, source_target_pairs={{0,1},{1,0},{2,3},{3,2},{4,5},{5,4},{6,7},{7,6},{8,9},{9,8},{10,11... | collective-permute-start | bytes 4718600 | tf_op jit(solution)/shard_map/ppermute | solution.py:35
  21.4 12.3 %collective-permute-start.1 = (f32[192,512]{1,0:T(8,128)S(1)}, f32[192,512]{1,0:T(8,128)S(1)}, u32[]{:S(2)}, u32[]{:S(2)}) collective-permute-start(f32[192,512]{1,0:T(8,128)S(1)} %get-tuple-element.61), channel_id=1, source_target_pairs={{0,4},{1,5},{2,6},{3,7},{4,0},{5,1},{6,2},{7,3},{8,12},{9,13},{10,... | collective-permute-start | bytes 1179656 | tf_op jit(solution)/shard_map/ppermute | solution.py:31
  24.3 18.0 %collective-permute-start.3 = (f32[192,512]{1,0:T(8,128)S(1)}, f32[192,512]{1,0:T(8,128)S(1)}, u32[]{:S(2)}, u32[]{:S(2)}) collective-permute-start(f32[192,512]{1,0:T(8,128)S(1)} %get-tuple-element.62), channel_id=1, source_target_pairs={{0,6},{1,7},{2,0},{3,1},{4,2},{5,3},{6,4},{7,5},{8,14},{9,15},{10,... | collective-permute-start | bytes 1179656 | tf_op jit(solution)/shard_map/ppermute | solution.py:31
  25.2 17.9 %collective-permute-start.2 = (f32[192,512]{1,0:T(8,128)S(1)}, f32[192,512]{1,0:T(8,128)}, u32[]{:S(2)}, u32[]{:S(2)}) collective-permute-start(f32[192,512]{1,0:T(8,128)S(1)} %get-tuple-element.63), channel_id=1, source_target_pairs={{0,2},{1,3},{2,4},{3,5},{4,6},{5,7},{6,0},{7,1},{8,10},{9,11},{10,... | collective-permute-start | bytes 1179656 | tf_op jit(solution)/shard_map/ppermute | solution.py:31
  33.7 8.6 %copy-start.12 = (f32[192,512]{1,0:T(8,128)}, f32[192,512]{1,0:T(8,128)S(1)}, u32[]{:S(2)}) copy-start(f32[192,512]{1,0:T(8,128)S(1)} %collective-permute-done.1) | copy-start | bytes 1179652
  42.3 0.7 copy-start.14
  43.1 1.0 copy-start.13
  43.1 1.1 copy-start.15
  45.3 25.8 %copy-start.6 = (f32[16,128]{1,0:T(8,128)S(1)}, f32[16,128]{1,0:T(8,128)}, u32[]{:S(2)}) copy-start(f32[16,128]{1,0:T(8,128)} %get-tuple-element.34.sq_one) | copy-start | bytes 24580
  45.3 25.8 %copy-start.7 = (f32[16,128]{1,0:T(8,128)S(1)}, f32[16,128]{1,0:T(8,128)}, u32[]{:S(2)}) copy-start(f32[16,128]{1,0:T(8,128)} %get-tuple-element.35.sq_two) | copy-start | bytes 24580
  45.3 11.2 %collective-permute-start.4 = (f32[192,512]{1,0:T(8,128)S(1)}, f32[192,512]{1,0:T(8,128)S(1)}, u32[]{:S(2)}, u32[]{:S(2)}) collective-permute-start(f32[192,512]{1,0:T(8,128)S(1)} %get-tuple-element.60), channel_id=1, source_target_pairs={{0,2},{1,3},{2,4},{3,5},{4,6},{5,7},{6,0},{7,1},{8,10},{9,11},{10,... | collective-permute-start | bytes 1179656 | tf_op jit(solution)/shard_map/ppermute | solution.py:31
  47.0 19.5 %collective-permute-start.5 = (f32[192,512]{1,0:T(8,128)S(1)}, f32[192,512]{1,0:T(8,128)S(1)}, u32[]{:S(2)}, u32[]{:S(2)}) collective-permute-start(f32[192,512]{1,0:T(8,128)S(1)} %get-tuple-element.60), channel_id=1, source_target_pairs={{0,4},{1,5},{2,6},{3,7},{4,0},{5,1},{6,2},{7,3},{8,12},{9,13},{10,... | collective-permute-start | bytes 1179656 | tf_op jit(solution)/shard_map/ppermute | solution.py:31
  49.3 17.2 %collective-permute-start.6 = (f32[192,512]{1,0:T(8,128)S(1)}, f32[192,512]{1,0:T(8,128)S(1)}, u32[]{:S(2)}, u32[]{:S(2)}) collective-permute-start(f32[192,512]{1,0:T(8,128)S(1)} %get-tuple-element.60), channel_id=1, source_target_pairs={{0,6},{1,7},{2,0},{3,1},{4,2},{5,3},{6,4},{7,5},{8,14},{9,15},{10,... | collective-permute-start | bytes 1179656 | tf_op jit(solution)/shard_map/ppermute | solution.py:31
  66.6 4.6 %collective-permute-start.7 = (f32[768,512]{1,0:T(8,128)S(1)}, f32[768,512]{1,0:T(8,128)}, u32[]{:S(2)}, u32[]{:S(2)}) collective-permute-start(f32[768,512]{1,0:T(8,128)S(1)} %constant_dynamic-update-slice_fusion.8.own), channel_id=1, source_target_pairs={{0,1},{1,0},{2,3},{3,2},{4,5},{5,4},{6,7},{7,6},{8,9},{9,8},{10,11... | collective-permute-start | bytes 4718600 | tf_op jit(solution)/shard_map/ppermute | solution.py:35
  83.4 0.8 copy-start.9
  84.2 0.8 copy-start.10
  85.0 14.5 %collective-permute-start.8 = (f32[32,3968]{1,0:T(8,128)}, f32[32,3968]{1,0:T(8,128)S(1)}, u32[]{:S(2)}, u32[]{:S(2)}) collective-permute-start(f32[32,3968]{1,0:T(8,128)} %get-tuple-element.37), channel_id=1, source_target_pairs={{0,16},{8,24},{16,0},{24,8},{32,48},{40,56},{48,32},{56,40},{64,80... | collective-permute-start | bytes 1523720 | tf_op jit(solution)/shard_map/ppermute | solution.py:31
  87.9 23.2 %collective-permute-start.9 = (f32[32,3968]{1,0:T(8,128)}, f32[32,3968]{1,0:T(8,128)S(1)}, u32[]{:S(2)}, u32[]{:S(2)}) collective-permute-start(f32[32,3968]{1,0:T(8,128)} %get-tuple-element.38), channel_id=1, source_target_pairs={{0,8},{8,16},{16,24},{24,0},{32,40},{40,48},{48,56},{56,32},{64,72... | collective-permute-start | bytes 1523720 | tf_op jit(solution)/shard_map/ppermute | solution.py:31
  88.3 22.8 %collective-permute-start.10 = (f32[32,3968]{1,0:T(8,128)}, f32[32,3968]{1,0:T(8,128)S(1)}, u32[]{:S(2)}, u32[]{:S(2)}) collective-permute-start(f32[32,3968]{1,0:T(8,128)} %get-tuple-element.39), channel_id=1, source_target_pairs={{0,24},{8,0},{16,8},{24,16},{32,56},{40,32},{48,40},{56,48},{64,88... | collective-permute-start | bytes 1523720 | tf_op jit(solution)/shard_map/ppermute | solution.py:31
  90.6 25.0 %collective-permute-start.14 = (f32[32,3968]{1,0:T(8,128)}, f32[32,3968]{1,0:T(8,128)S(1)}, u32[]{:S(2)}, u32[]{:S(2)}) collective-permute-start(f32[32,3968]{1,0:T(8,128)} %copy-done.10), channel_id=1, source_target_pairs={{0,64},{8,72},{16,80},{24,88},{32,96},{40,104},{48,112},{56,120},{... | collective-permute-start | bytes 1523720 | tf_op jit(solution)/shard_map/ppermute | solution.py:31
  94.2 24.2 %collective-permute-start.15 = (f32[32,3968]{1,0:T(8,128)}, f32[32,3968]{1,0:T(8,128)S(1)}, u32[]{:S(2)}, u32[]{:S(2)}) collective-permute-start(f32[32,3968]{1,0:T(8,128)} %copy-done.9), channel_id=1, source_target_pairs={{0,32},{8,40},{16,48},{24,56},{32,64},{40,72},{48,80},{56,88},{64,... | collective-permute-start | bytes 1523720 | tf_op jit(solution)/shard_map/ppermute | solution.py:31
  99.5 18.9 %collective-permute-start.16 = (f32[32,3968]{1,0:T(8,128)S(1)}, f32[32,3968]{1,0:T(8,128)S(1)}, u32[]{:S(2)}, u32[]{:S(2)}) collective-permute-start(f32[32,3968]{1,0:T(8,128)S(1)} %get-tuple-element.43), channel_id=1, source_target_pairs={{0,96},{8,104},{16,112},{24,120},{32,0},{40,8},{48,16},{56,24},{64... | collective-permute-start | bytes 1523720 | tf_op jit(solution)/shard_map/ppermute | solution.py:31
  111.2 9.3 %collective-permute-start.11 = (f32[8,3968]{1,0:T(8,128)S(1)}, f32[8,3968]{1,0:T(8,128)S(1)}, u32[]{:S(2)}, u32[]{:S(2)}) collective-permute-start(f32[8,3968]{1,0:T(8,128)S(1)} %get-tuple-element.69), channel_id=1, source_target_pairs={{0,64},{8,72},{16,80},{24,88},{32,96},{40,104},{48,112},{56,120},{... | collective-permute-start | bytes 380936 | tf_op jit(solution)/shard_map/ppermute | solution.py:31
  115.0 7.5 %collective-permute-start.13 = (f32[8,3968]{1,0:T(8,128)S(1)}, f32[8,3968]{1,0:T(8,128)S(1)}, u32[]{:S(2)}, u32[]{:S(2)}) collective-permute-start(f32[8,3968]{1,0:T(8,128)S(1)} %get-tuple-element.70), channel_id=1, source_target_pairs={{0,96},{8,104},{16,112},{24,120},{32,0},{40,8},{48,16},{56,24},{64... | collective-permute-start | bytes 380936 | tf_op jit(solution)/shard_map/ppermute | solution.py:31
  115.6 6.8 %collective-permute-start.12 = (f32[8,3968]{1,0:T(8,128)S(1)}, f32[8,3968]{1,0:T(8,128)S(1)}, u32[]{:S(2)}, u32[]{:S(2)}) collective-permute-start(f32[8,3968]{1,0:T(8,128)S(1)} %get-tuple-element.71), channel_id=1, source_target_pairs={{0,32},{8,40},{16,48},{24,56},{32,64},{40,72},{48,80},{56,88},{64,... | collective-permute-start | bytes 380936 | tf_op jit(solution)/shard_map/ppermute | solution.py:31
  118.6 5.4 %collective-permute-start.17 = (f32[8,3968]{1,0:T(8,128)S(1)}, f32[8,3968]{1,0:T(8,128)S(1)}, u32[]{:S(2)}, u32[]{:S(2)}) collective-permute-start(f32[8,3968]{1,0:T(8,128)S(1)} %get-tuple-element.66), channel_id=1, source_target_pairs={{0,16},{8,24},{16,0},{24,8},{32,48},{40,56},{48,32},{56,40},{64,80... | collective-permute-start | bytes 380936 | tf_op jit(solution)/shard_map/ppermute | solution.py:31
  118.7 6.1 %collective-permute-start.19 = (f32[8,3968]{1,0:T(8,128)S(1)}, f32[8,3968]{1,0:T(8,128)S(1)}, u32[]{:S(2)}, u32[]{:S(2)}) collective-permute-start(f32[8,3968]{1,0:T(8,128)S(1)} %get-tuple-element.67), channel_id=1, source_target_pairs={{0,24},{8,0},{16,8},{24,16},{32,56},{40,32},{48,40},{56,48},{64,88... | collective-permute-start | bytes 380936 | tf_op jit(solution)/shard_map/ppermute | solution.py:31
  120.6 6.6 %collective-permute-start.18 = (f32[8,3968]{1,0:T(8,128)S(1)}, f32[8,3968]{1,0:T(8,128)S(1)}, u32[]{:S(2)}, u32[]{:S(2)}) collective-permute-start(f32[8,3968]{1,0:T(8,128)S(1)} %get-tuple-element.68), channel_id=1, source_target_pairs={{0,8},{8,16},{16,24},{24,0},{32,40},{40,48},{48,56},{56,32},{64,72... | collective-permute-start | bytes 380936 | tf_op jit(solution)/shard_map/ppermute | solution.py:31
  127.9 145.4 %all-gather.3.cloned.1.call-start = ((), (), s32[]{:S(2)}) async-start(), calls=%async_computation.1 | async-start | bytes 3342336 | tf_op jit(solution)/shard_map/all_gather | solution.py:577
  128.0 6.2 %collective-permute-start.20 = (f32[48,256]{1,0:T(8,128)S(1)}, f32[48,256]{1,0:T(8,128)S(1)}, u32[]{:S(2)}, u32[]{:S(2)}) collective-permute-start(f32[48,256]{1,0:T(8,128)S(1)} %pad_maximum_fusion.4), channel_id=1, source_target_pairs={{0,0},{1,16},{2,32},{3,48},{4,64},{5,80},{6,96},{7,112},{8,2},{9,1... | collective-permute-start | bytes 147464 | tf_op jit(solution)/shard_map/ppermute | solution.py:117
  134.1 10.6 %collective-permute-start.23 = (f32[48,256]{1,0:T(8,128)S(1)}, f32[48,256]{1,0:T(8,128)S(1)}, u32[]{:S(2)}, u32[]{:S(2)}) collective-permute-start(f32[48,256]{1,0:T(8,128)S(1)} %collective-permute-done.20), channel_id=1, source_target_pairs={{0,6},{1,7},{2,0},{3,1},{4,2},{5,3},{6,4},{7,5},{8,14},{9,15},{10,... | collective-permute-start | bytes 147464 | tf_op jit(solution)/shard_map/ppermute | solution.py:31
  140.0 4.7 %collective-permute-start.22 = (f32[48,256]{1,0:T(8,128)S(1)}, f32[48,256]{1,0:T(8,128)S(1)}, u32[]{:S(2)}, u32[]{:S(2)}) collective-permute-start(f32[48,256]{1,0:T(8,128)S(1)} %collective-permute-done.20), channel_id=1, source_target_pairs={{0,4},{1,5},{2,6},{3,7},{4,0},{5,1},{6,2},{7,3},{8,12},{9,13},{10,... | collective-permute-start | bytes 147464 | tf_op jit(solution)/shard_map/ppermute | solution.py:31
  140.0 4.7 %collective-permute-start.21 = (f32[48,256]{1,0:T(8,128)S(1)}, f32[48,256]{1,0:T(8,128)S(1)}, u32[]{:S(2)}, u32[]{:S(2)}) collective-permute-start(f32[48,256]{1,0:T(8,128)S(1)} %collective-permute-done.20), channel_id=1, source_target_pairs={{0,2},{1,3},{2,4},{3,5},{4,6},{5,7},{6,0},{7,1},{8,10},{9,11},{10,... | collective-permute-start | bytes 147464 | tf_op jit(solution)/shard_map/ppermute | solution.py:31
  144.7 3.9 %collective-permute-start.24 = (f32[192,256]{1,0:T(8,128)S(1)}, f32[192,256]{1,0:T(8,128)S(1)}, u32[]{:S(2)}, u32[]{:S(2)}) collective-permute-start(f32[192,256]{1,0:T(8,128)S(1)} %constant_dynamic-update-slice_fusion.4), channel_id=1, source_target_pairs={{0,1},{1,0},{2,3},{3,2},{4,5},{5,4},{6,7},{7,6},{8,9},{9,8},{10,11... | collective-permute-start | bytes 589832 | tf_op jit(solution)/shard_map/ppermute | solution.py:35
  148.7 5.6 %copy-start.1 = (f32[384,256]{1,0:T(8,128)}, f32[384,256]{1,0:T(8,128)S(1)}, u32[]{:S(2)}) copy-start(f32[384,256]{1,0:T(8,128)S(1)} %pad_maximum_fusion.2.rows_act) | copy-start | bytes 1179652
  154.3 14.9 %collective-permute-start.25 = (f32[32,3072]{1,0:T(8,128)S(1)}, f32[32,3072]{1,0:T(8,128)S(1)}, u32[]{:S(2)}, u32[]{:S(2)}) collective-permute-start(f32[32,3072]{1,0:T(8,128)S(1)} %get-tuple-element.45), channel_id=1, source_target_pairs={{0,16},{8,24},{16,0},{24,8},{32,48},{40,56},{48,32},{56,40},{64,80... | collective-permute-start | bytes 1179656 | tf_op jit(solution)/shard_map/ppermute | solution.py:31
  154.7 29.0 %collective-permute-start.26 = (f32[32,3072]{1,0:T(8,128)S(1)}, f32[32,3072]{1,0:T(8,128)S(1)}, u32[]{:S(2)}, u32[]{:S(2)}) collective-permute-start(f32[32,3072]{1,0:T(8,128)S(1)} %get-tuple-element.46), channel_id=1, source_target_pairs={{0,8},{8,16},{16,24},{24,0},{32,40},{40,48},{48,56},{56,32},{64,72... | collective-permute-start | bytes 1179656 | tf_op jit(solution)/shard_map/ppermute | solution.py:31
  156.9 27.0 %collective-permute-start.27 = (f32[32,3072]{1,0:T(8,128)S(1)}, f32[32,3072]{1,0:T(8,128)S(1)}, u32[]{:S(2)}, u32[]{:S(2)}) collective-permute-start(f32[32,3072]{1,0:T(8,128)S(1)} %get-tuple-element.47), channel_id=1, source_target_pairs={{0,24},{8,0},{16,8},{24,16},{32,56},{40,32},{48,40},{56,48},{64,88... | collective-permute-start | bytes 1179656 | tf_op jit(solution)/shard_map/ppermute | solution.py:31
  158.8 33.5 %collective-permute-start.31 = (f32[32,3072]{1,0:T(8,128)S(1)}, f32[32,3072]{1,0:T(8,128)S(1)}, u32[]{:S(2)}, u32[]{:S(2)}) collective-permute-start(f32[32,3072]{1,0:T(8,128)S(1)} %get-tuple-element.49), channel_id=1, source_target_pairs={{0,64},{8,72},{16,80},{24,88},{32,96},{40,104},{48,112},{56,120},{... | collective-permute-start | bytes 1179656 | tf_op jit(solution)/shard_map/ppermute | solution.py:31
  160.4 32.5 %collective-permute-start.32 = (f32[32,3072]{1,0:T(8,128)S(1)}, f32[32,3072]{1,0:T(8,128)S(1)}, u32[]{:S(2)}, u32[]{:S(2)}) collective-permute-start(f32[32,3072]{1,0:T(8,128)S(1)} %get-tuple-element.50), channel_id=1, source_target_pairs={{0,32},{8,40},{16,48},{24,56},{32,64},{40,72},{48,80},{56,88},{64,... | collective-permute-start | bytes 1179656 | tf_op jit(solution)/shard_map/ppermute | solution.py:31
  169.2 25.2 %collective-permute-start.33 = (f32[32,3072]{1,0:T(8,128)S(1)}, f32[32,3072]{1,0:T(8,128)S(1)}, u32[]{:S(2)}, u32[]{:S(2)}) collective-permute-start(f32[32,3072]{1,0:T(8,128)S(1)} %get-tuple-element.51), channel_id=1, source_target_pairs={{0,96},{8,104},{16,112},{24,120},{32,0},{40,8},{48,16},{56,24},{64... | collective-permute-start | bytes 1179656 | tf_op jit(solution)/shard_map/ppermute | solution.py:31
  184.0 14.0 %collective-permute-start.28 = (f32[8,3072]{1,0:T(8,128)S(1)}, f32[8,3072]{1,0:T(8,128)S(1)}, u32[]{:S(2)}, u32[]{:S(2)}) collective-permute-start(f32[8,3072]{1,0:T(8,128)S(1)} %get-tuple-element.75), channel_id=1, source_target_pairs={{0,64},{8,72},{16,80},{24,88},{32,96},{40,104},{48,112},{56,120},{... | collective-permute-start | bytes 294920 | tf_op jit(solution)/shard_map/ppermute | solution.py:31
  186.2 12.4 %collective-permute-start.30 = (f32[8,3072]{1,0:T(8,128)S(1)}, f32[8,3072]{1,0:T(8,128)S(1)}, u32[]{:S(2)}, u32[]{:S(2)}) collective-permute-start(f32[8,3072]{1,0:T(8,128)S(1)} %get-tuple-element.76), channel_id=1, source_target_pairs={{0,96},{8,104},{16,112},{24,120},{32,0},{40,8},{48,16},{56,24},{64... | collective-permute-start | bytes 294920 | tf_op jit(solution)/shard_map/ppermute | solution.py:31
  192.3 6.7 %collective-permute-start.29 = (f32[8,3072]{1,0:T(8,128)S(1)}, f32[8,3072]{1,0:T(8,128)S(1)}, u32[]{:S(2)}, u32[]{:S(2)}) collective-permute-start(f32[8,3072]{1,0:T(8,128)S(1)} %get-tuple-element.77), channel_id=1, source_target_pairs={{0,32},{8,40},{16,48},{24,56},{32,64},{40,72},{48,80},{56,88},{64,... | collective-permute-start | bytes 294920 | tf_op jit(solution)/shard_map/ppermute | solution.py:31
  194.5 5.1 %collective-permute-start.34 = (f32[8,3072]{1,0:T(8,128)S(1)}, f32[8,3072]{1,0:T(8,128)S(1)}, u32[]{:S(2)}, u32[]{:S(2)}) collective-permute-start(f32[8,3072]{1,0:T(8,128)S(1)} %get-tuple-element.78), channel_id=1, source_target_pairs={{0,16},{8,24},{16,0},{24,8},{32,48},{40,56},{48,32},{56,40},{64,80... | collective-permute-start | bytes 294920 | tf_op jit(solution)/shard_map/ppermute | solution.py:31
  197.2 3.5 %collective-permute-start.36 = (f32[8,3072]{1,0:T(8,128)S(1)}, f32[8,3072]{1,0:T(8,128)S(1)}, u32[]{:S(2)}, u32[]{:S(2)}) collective-permute-start(f32[8,3072]{1,0:T(8,128)S(1)} %get-tuple-element.79), channel_id=1, source_target_pairs={{0,24},{8,0},{16,8},{24,16},{32,56},{40,32},{48,40},{56,48},{64,88... | collective-permute-start | bytes 294920 | tf_op jit(solution)/shard_map/ppermute | solution.py:31
  198.1 5.5 %collective-permute-start.35 = (f32[8,3072]{1,0:T(8,128)S(1)}, f32[8,3072]{1,0:T(8,128)S(1)}, u32[]{:S(2)}, u32[]{:S(2)}) collective-permute-start(f32[8,3072]{1,0:T(8,128)S(1)} %get-tuple-element.80), channel_id=1, source_target_pairs={{0,8},{8,16},{16,24},{24,0},{32,40},{40,48},{48,56},{56,32},{64,72... | collective-permute-start | bytes 294920 | tf_op jit(solution)/shard_map/ppermute | solution.py:31
  213.1 15.6 %copy-start.4 = (f32[64,256]{1,0:T(8,128)S(1)}, f32[64,256]{1,0:T(8,128)}, u32[]{:S(2)}) copy-start(f32[64,256]{1,0:T(8,128)} %get-tuple-element.53.cores) | copy-start | bytes 196612
  213.1 15.6 %copy-start.5 = (f32[16,256]{1,0:T(8,128)S(1)}, f32[16,256]{1,0:T(8,128)}, u32[]{:S(2)}) copy-start(f32[16,256]{1,0:T(8,128)} %get-tuple-element.54.both) | copy-start | bytes 49156
  213.1 5.4 %collective-permute-start.37 = (f32[480,256]{1,0:T(8,128)S(1)}, f32[480,256]{1,0:T(8,128)S(1)}, u32[]{:S(2)}, u32[]{:S(2)}) collective-permute-start(f32[480,256]{1,0:T(8,128)S(1)} %constant_dynamic-slice_fusion.3), channel_id=1, source_target_pairs={{0,1},{1,0},{2,3},{3,2},{4,5},{5,4},{6,7},{7,6},{8,9},{9,8},{10,11... | collective-permute-start | bytes 1474568 | tf_op jit(solution)/shard_map/ppermute | solution.py:35
  219.7 6.1 %collective-permute-start.38 = (f32[120,256]{1,0:T(8,128)S(1)}, f32[120,256]{1,0:T(8,128)S(1)}, u32[]{:S(2)}, u32[]{:S(2)}) collective-permute-start(f32[120,256]{1,0:T(8,128)S(1)} %get-tuple-element.72), channel_id=1, source_target_pairs={{0,4},{1,5},{2,6},{3,7},{4,0},{5,1},{6,2},{7,3},{8,12},{9,13},{10,... | collective-permute-start | bytes 368648 | tf_op jit(solution)/shard_map/ppermute | solution.py:31
  220.4 5.8 %collective-permute-start.40 = (f32[120,256]{1,0:T(8,128)S(1)}, f32[120,256]{1,0:T(8,128)S(1)}, u32[]{:S(2)}, u32[]{:S(2)}) collective-permute-start(f32[120,256]{1,0:T(8,128)S(1)} %get-tuple-element.73), channel_id=1, source_target_pairs={{0,6},{1,7},{2,0},{3,1},{4,2},{5,3},{6,4},{7,5},{8,14},{9,15},{10,... | collective-permute-start | bytes 368648 | tf_op jit(solution)/shard_map/ppermute | solution.py:31
  221.4 7.3 %collective-permute-start.39 = (f32[120,256]{1,0:T(8,128)S(1)}, f32[120,256]{1,0:T(8,128)S(1)}, u32[]{:S(2)}, u32[]{:S(2)}) collective-permute-start(f32[120,256]{1,0:T(8,128)S(1)} %get-tuple-element.74), channel_id=1, source_target_pairs={{0,2},{1,3},{2,4},{3,5},{4,6},{5,7},{6,0},{7,1},{8,10},{9,11},{10,... | collective-permute-start | bytes 368648 | tf_op jit(solution)/shard_map/ppermute | solution.py:31
  229.0 0.6 copy-start.8
  229.5 15.2 %collective-permute-start.41 = (f32[128,256]{1,0:T(8,128)S(1)}, f32[128,256]{1,0:T(8,128)S(1)}, u32[]{:S(2)}, u32[]{:S(2)}) collective-permute-start(f32[128,256]{1,0:T(8,128)S(1)} %get-tuple-element.55), channel_id=1, source_target_pairs={{0,2},{1,3},{2,4},{3,5},{4,6},{5,7},{6,0},{7,1},{8,10},{9,11},{10,... | collective-permute-start | bytes 393224 | tf_op jit(solution)/shard_map/ppermute | solution.py:31
  239.5 8.0 %collective-permute-start.43 = (f32[128,256]{1,0:T(8,128)S(1)}, f32[128,256]{1,0:T(8,128)S(1)}, u32[]{:S(2)}, u32[]{:S(2)}) collective-permute-start(f32[128,256]{1,0:T(8,128)S(1)} %get-tuple-element.55), channel_id=1, source_target_pairs={{0,6},{1,7},{2,0},{3,1},{4,2},{5,3},{6,4},{7,5},{8,14},{9,15},{10,... | collective-permute-start | bytes 393224 | tf_op jit(solution)/shard_map/ppermute | solution.py:31
  242.1 5.4 %collective-permute-start.42 = (f32[128,256]{1,0:T(8,128)S(1)}, f32[128,256]{1,0:T(8,128)S(1)}, u32[]{:S(2)}, u32[]{:S(2)}) collective-permute-start(f32[128,256]{1,0:T(8,128)S(1)} %get-tuple-element.55), channel_id=1, source_target_pairs={{0,4},{1,5},{2,6},{3,7},{4,0},{5,1},{6,2},{7,3},{8,12},{9,13},{10,... | collective-permute-start | bytes 393224 | tf_op jit(solution)/shard_map/ppermute | solution.py:31
  247.5 4.2 %collective-permute-start.44 = (f32[512,256]{1,0:T(8,128)S(1)}, f32[512,256]{1,0:T(8,128)S(1)}, u32[]{:S(2)}, u32[]{:S(2)}) collective-permute-start(f32[512,256]{1,0:T(8,128)S(1)} %constant_dynamic-update-slice_fusion), channel_id=1, source_target_pairs={{0,1},{1,0},{2,3},{3,2},{4,5},{5,4},{6,7},{7,6},{8,9},{9,8},{10,11... | collective-permute-start | bytes 1572872 | tf_op jit(solution)/shard_map/ppermute | solution.py:35
  251.9 21.5 %copy-start = (f32[1024,256]{1,0:T(8,128)}, f32[1024,256]{1,0:T(8,128)S(1)}, u32[]{:S(2)}) copy-start(f32[1024,256]{1,0:T(8,128)S(1)} %pad_maximum_fusion.right) | copy-start | bytes 3145732
  252.7 20.6 %all-to-all-start = ((f32[16,16,256]{2,1,0:T(8,128)}), f32[16,16,256]{2,1,0:T(8,128)S(1)}, u32[]{:S(2)}, u32[]{:S(2)}) async-start(f32[16,16,256]{2,1,0:T(8,128)} %bitcast.5), calls=%async_computation | async-start | bytes 524288 | tf_op jit(solution)/shard_map/all_to_all | solution.py:583
  271.9 0.7 copy-start.2
  272.6 0.7 copy-start.3
  273.3 0.7 copy-start.11
Sparse Core Ops, SparseCore 0:
  128.0 69.1 all-gather.4
  204.4 48.3 all-gather.2
